TPU v7x, 256 devices: a whole 4x4x8 slice. The times are simulated.
256 devices in a mesh: dp: 2 (over y_lo), ctx: 32 (over z, y_hi, core), mp: 4 (over x).
Axes of the slice: x: 4, y: 4 (y_hi: 2, y_lo: 2; y = y_hi * 2 + y_lo), z: 8, core: 2. Of those that a mesh axis runs over, the one named last changes fastest.
Arguments:
- queries: bfloat16 [2, 4096, 2048], P('dp', 'ctx', 'mp'), may hold values from -6 to 6
- key_rows: bfloat16 [2, 4096, 2048], P('dp', 'ctx', 'mp'), may hold values from -6 to 6
- value_rows: bfloat16 [2, 4096, 2048], P('dp', 'ctx', 'mp'), may hold values from -6 to 6
- out_weight: bfloat16 [4096, 2048], P(('dp', 'ctx'), 'mp'), may hold values from -0.125 to 0.125
- out_grad: bfloat16 [2, 4096, 4096], P('dp', 'ctx', 'mp'), may hold values from -1.5 to 1.5
- block_offsets: int32 [2, 32], P('dp'), may hold values from 0 to 31, each once within a row
Outputs:
- projected: bfloat16 [2, 4096, 4096], P('dp', 'ctx', 'mp')
- query_grad: bfloat16 [2, 4096, 2048], P('dp', 'ctx', 'mp')
- key_grad: bfloat16 [2, 4096, 2048], P('dp', 'ctx', 'mp')
- value_grad: bfloat16 [2, 4096, 2048], P('dp', 'ctx', 'mp')
- weight_grad: float32 [4096, 2048], P(('dp', 'ctx'), 'mp')
Inputs may be any that keep to these rules, and one draw needn't show every extreme that they name: Each row of block_offsets is a permutation of 0 to 31.
All inputs are finite; a program needn't handle non-finite values.
Results may differ from a plain program's by a relative error of at most 0.04.
Values may be sent and summed in bfloat16 or wider, within the bound.
A program may use at most 128 MiB of HBM per device.

v0:
```python
import math

import jax
import jax.numpy as jnp
from jax import lax
from jax.sharding import PartitionSpec as P

HD = 128


MASKED = -1e30


def row_positions(first_row, piece_rows, offsets, tok_rows):
    row_ids = first_row + jnp.arange(piece_rows, dtype=jnp.int32)
    blocks = row_ids // tok_rows
    block_ids = jnp.arange(offsets.shape[0], dtype=jnp.int32)
    picked = jnp.sum(jnp.where(blocks[:, None] == block_ids[None, :], offsets[None, :], 0), axis=1)
    return picked * tok_rows + row_ids % tok_rows


def on_device(queries, key_rows, value_rows, out_weight, out_grad, block_offsets):
    tok_rows = queries.shape[1]
    all_width = queries.shape[2]
    head_count = all_width // HD
    score_scale = HD ** (-0.5)
    ctx_size = lax.axis_size("ctx")
    seq_len = tok_rows * ctx_size
    offsets = block_offsets[0]
    query_pos = row_positions(lax.axis_index("ctx") * tok_rows, tok_rows, offsets, tok_rows)
    query_heads = queries[0].reshape(tok_rows, head_count, HD)
    own_keys = key_rows[0]
    own_values = value_rows[0]
    row_top = jnp.full((head_count, tok_rows), MASKED, jnp.float32)
    key_piece = lax.all_gather(own_keys, "ctx", axis=0, tiled=True)
    value_piece = lax.all_gather(own_values, "ctx", axis=0, tiled=True)
    piece_rows = key_piece.shape[0]
    allowed = (
        row_positions(jnp.int32(0), piece_rows, offsets, tok_rows)[None, :] <= query_pos[:, None]
    )
    old_top = row_top
    scores = (
        jnp.einsum(
            "thd,nhd->htn",
            query_heads,
            key_piece.reshape(piece_rows, head_count, HD),
            preferred_element_type=jnp.float32,
        )
        * score_scale
    )
    scores = jnp.where(allowed[None], scores, MASKED)
    new_top = jnp.maximum(old_top, jnp.max(scores, axis=2))
    raised = jnp.where(allowed[None], jnp.exp(scores - new_top[:, :, None]), 0.0)
    new_total = jnp.sum(raised, axis=2)
    new_weighted = jnp.einsum(
        "htn,nhd->htd",
        raised.astype(jnp.bfloat16),
        value_piece.reshape(piece_rows, head_count, HD),
        preferred_element_type=jnp.float32,
    )
    running = (new_top, new_total, new_weighted)
    row_top, row_total, weighted, key_all, value_all = running + (key_piece, value_piece)
    attended = (
        (weighted / row_total[:, :, None])
        .transpose(1, 0, 2)
        .reshape(tok_rows, all_width)
        .astype(jnp.bfloat16)
    )
    log_total = (row_top + jnp.log(row_total)).T
    portion = lax.all_gather(out_weight, ("dp", "ctx"), axis=0, tiled=True)
    partial_out = jnp.dot(attended, portion.T, preferred_element_type=jnp.float32)
    weight_cols = portion.T
    projected = lax.psum_scatter(
        partial_out.astype(jnp.bfloat16), "mp", scatter_dimension=1, tiled=True
    )
    grad_full = lax.all_gather(out_grad[0], "mp", axis=1, tiled=True)
    grad_flat = jnp.einsum(
        "td,wd->tw", grad_full, weight_cols, preferred_element_type=jnp.float32
    ).astype(jnp.bfloat16)
    grad_heads = grad_flat.reshape(tok_rows, head_count, HD)
    attn_heads = attended.reshape(tok_rows, head_count, HD)
    row_delta = jnp.sum(grad_heads.astype(jnp.float32) * attn_heads.astype(jnp.float32), axis=2)
    lse_all, delta_all = (
        lax.all_gather(log_total, "ctx", axis=0, tiled=True),
        lax.all_gather(row_delta, "ctx", axis=0, tiled=True),
    )
    key_span = math.gcd(seq_len, 512)
    block_count = seq_len // key_span
    own_lse = log_total.T
    own_delta = row_delta.T

    def query_step(query_acc, block_items):
        key_block, value_block, number = block_items
        allowed = (
            row_positions(number * key_span, key_span, offsets, tok_rows)[None, :]
            <= query_pos[:, None]
        )
        key_heads = key_block.reshape(key_span, head_count, HD)
        value_heads = value_block.reshape(key_span, head_count, HD)
        scores = (
            jnp.einsum("thd,nhd->htn", query_heads, key_heads, preferred_element_type=jnp.float32)
            * score_scale
        )
        attn_prob = jnp.where(allowed[None], jnp.exp(scores - own_lse[:, :, None]), 0.0)
        prob_grad = jnp.einsum(
            "thd,nhd->htn", grad_heads, value_heads, preferred_element_type=jnp.float32
        )
        score_grad = (attn_prob * (prob_grad - own_delta[:, :, None]) * score_scale).astype(
            jnp.bfloat16
        )
        query_acc = query_acc + jnp.einsum(
            "htn,nhd->thd", score_grad, key_heads, preferred_element_type=jnp.float32
        )
        return (query_acc, None)

    query_acc, unused = lax.scan(
        query_step,
        jnp.zeros((tok_rows, head_count, HD), jnp.float32),
        (
            key_all.reshape(block_count, key_span, all_width),
            value_all.reshape(block_count, key_span, all_width),
            jnp.arange(block_count, dtype=jnp.int32),
        ),
    )
    own_key_heads = own_keys.reshape(tok_rows, head_count, HD)
    own_value_heads = own_values.reshape(tok_rows, head_count, HD)
    query_piece = lax.all_gather(queries[0], "ctx", axis=0, tiled=True)
    grad_piece = lax.all_gather(grad_flat, "ctx", axis=0, tiled=True)
    piece_rows = query_piece.shape[0]
    allowed = (
        query_pos[None, :] <= row_positions(jnp.int32(0), piece_rows, offsets, tok_rows)[:, None]
    )
    lse_piece = lse_all.T
    delta_piece = delta_all.T
    query_part = query_piece.reshape(piece_rows, head_count, HD)
    grad_part = grad_piece.reshape(piece_rows, head_count, HD)
    scores = (
        jnp.einsum("nhd,khd->hnk", query_part, own_key_heads, preferred_element_type=jnp.float32)
        * score_scale
    )
    attn_prob = jnp.where(allowed[None], jnp.exp(scores - lse_piece[:, :, None]), 0.0)
    value_acc = jnp.einsum(
        "hnk,nhd->khd",
        attn_prob.astype(jnp.bfloat16),
        grad_part,
        preferred_element_type=jnp.float32,
    )
    prob_grad = jnp.einsum(
        "nhd,khd->hnk", grad_part, own_value_heads, preferred_element_type=jnp.float32
    )
    score_grad = (attn_prob * (prob_grad - delta_piece[:, :, None]) * score_scale).astype(
        jnp.bfloat16
    )
    key_acc = jnp.einsum("hnk,nhd->khd", score_grad, query_part, preferred_element_type=jnp.float32)
    key_acc, value_acc = (key_acc, value_acc)
    weight_grad = lax.psum_scatter(
        lax.dot_general(
            grad_full, attended, (((0,), (0,)), ((), ())), preferred_element_type=jnp.float32
        ),
        ("dp", "ctx"),
        scatter_dimension=0,
        tiled=True,
    )
    query_grad = query_acc.reshape(tok_rows, all_width).astype(jnp.bfloat16)
    key_grad = key_acc.reshape(tok_rows, all_width).astype(jnp.bfloat16)
    value_grad = value_acc.reshape(tok_rows, all_width).astype(jnp.bfloat16)
    return (projected[None], query_grad[None], key_grad[None], value_grad[None], weight_grad)


def solution(mesh):
    placed = (
        P("dp", "ctx", "mp"),
        P("dp", "ctx", "mp"),
        P("dp", "ctx", "mp"),
        P(("dp", "ctx"), "mp"),
        P("dp", "ctx", "mp"),
        P("dp", None),
    )
    return jax.shard_map(
        on_device,
        mesh=mesh,
        in_specs=placed,
        out_specs=(
            P("dp", "ctx", "mp"),
            P("dp", "ctx", "mp"),
            P("dp", "ctx", "mp"),
            P("dp", "ctx", "mp"),
            P(("dp", "ctx"), "mp"),
        ),
        check_vma=False,
    )
```

profile of v0, /device:TPU:1, one launch (start us, length us, event | category | flops | bytes accessed | tf_op | source)
XLA Modules:
  0.0 815.9 jit_solution(15279405716518977509)
XLA Ops:
  9.4 1.7 copy.107
  11.2 1.7 copy.106
  12.9 26.3 %all-gather.19.cloned.1.call-done = bf16[1,128,4096]{2,1,0:T(8,128)(2,1)} async-done(((bf16[1,128,1024]{2,1,0:T(8,128)(2,1)}), bf16[1,128,4096]{2,1,0:T(8,128)(2,1)}) %all-gather.19.cloned.1.call-update) | async-done | bytes 1048592 | tf_op jit(solution)/shard_map/all_gather | solution.py:76
  39.2 119.8 %all-gather.11.cloned.1.call-done = bf16[4096,512]{1,0:T(8,128)(2,1)} async-done(((bf16[64,512]{1,0:T(8,128)(2,1)}), bf16[4096,512]{1,0:T(8,128)(2,1)}) %all-gather.11.cloned.1.call-update) | async-done | bytes 4194320 | tf_op jit(solution)/shard_map/all_gather | solution.py:70
  159.0 3.9 convolution_convert_fusion.1
  163.7 83.2 %all-gather.17.cloned.1.call-done = bf16[1,4096,512]{2,1,0:T(8,128)(2,1)} async-done(((bf16[1,128,512]{2,1,0:T(8,128)(2,1)}), bf16[1,4096,512]{2,1,0:T(8,128)(2,1)}) %all-gather.17.cloned.1.call-update) | async-done | bytes 4194320 | tf_op jit(solution)/shard_map/all_gather | solution.py:36
  247.0 6.4 copy.110
  253.3 80.2 %all-gather.15.cloned.1.call-done = bf16[1,4096,512]{1,2,0:T(8,128)(2,1)} async-done(((bf16[1,128,512]{1,2,0:T(8,128)(2,1)}), bf16[1,4096,512]{1,2,0:T(8,128)(2,1)}) %all-gather.15.cloned.1.call-update) | async-done | bytes 4194320 | tf_op jit(solution)/shard_map/all_gather | solution.py:35
  333.6 4.3 fusion.18
  337.9 3.2 copy-done
  341.1 2.5 fusion.19
  343.7 7.3 multiply_reduce_fusion
  351.1 2.5 convolution_convert_fusion
  353.6 4.5 convolution_bitcast_fusion
  358.1 9.0 %copy.134 = f32[4096,512]{1,0:T(8,128)} copy(f32[4096,512]{0,1:T(8,128)} %convolution_bitcast_fusion) | data formatting | bytes 16777216
  368.2 1.9 broadcast_compare_fusion.1
  370.0 6.5 copy.111
  376.5 39.7 %all_gather.29 = f32[4096,4]{0,1:T(4,128)S(1)} all-gather(f32[128,4]{0,1:T(4,128)S(1)} %bitcast_add_fusion), channel_id=1, replica_groups=mesh['dp'=2,'ctx'=32,'mp'=4] {'ctx'}, dimensions={0}, use_global_device_ids=true | all-gather | bytes 67584 | tf_op jit(solution)/shard_map/all_gather | solution.py:84
  416.2 4.4 all-gather.21.cloned.1.call-done
  420.6 7.8 exponential_select_fusion
  428.6 34.0 %while.13 = (s32[]{:T(128)}, f32[128,4,128]{0,2,1:T(8,128)S(1)}, bf16[8,512,512]{2,1,0:T(8,128)(2,1)}, s32[8]{0:T(128)S(1)}, s32[1,32]{1,0:T(1,128)S(1)}, /*inde...) while((s32[]{:T(128)}, f32[128,4,128]{0,2,1:T(8,128)S(1)}, ...), condition=%wide.region_8.9_spmd.clone, body=%wide.region_6.8_spmd.clone.sunk | while | flops 203422208 | bytes 8799035 | solution.py:116
  432.8 1.3 constant_dynamic-slice_fusion.3
  437.1 1.3 constant_dynamic-slice_fusion.3
  441.3 1.3 constant_dynamic-slice_fusion.3
  445.6 1.3 constant_dynamic-slice_fusion.3
  463.3 39.6 %all_gather.31 = f32[4096,4]{0,1:T(4,128)S(1)} all-gather(f32[128,4]{0,1:T(4,128)S(1)} %bitcast.127), channel_id=1, replica_groups=mesh['dp'=2,'ctx'=32,'mp'=4] {'ctx'}, dimensions={0}, use_global_device_ids=true | all-gather | bytes 67584 | tf_op jit(solution)/shard_map/all_gather | solution.py:85
  503.0 4.5 all-gather.13.cloned.1.call-done
  507.5 6.4 copy.138
  513.9 8.0 fusion.33
  522.7 6.0 fusion.30
  529.5 2.0 reduce-scatter.5.cloned.1.call-done
  531.6 277.5 %reduce-scatter.7.cloned.1.call-done = f32[64,512]{1,0:T(8,128)} async-done(((f32[4096,512]{1,0:T(8,128)}), f32[64,512]{1,0:T(8,128)}) %reduce-scatter.7.cloned.1.call-update) | async-done | bytes 131088
  (128 shorter events, 29.8 us)
Async XLA Ops:
  7.2 155.9 %copy-start.7 = (s32[1,32]{1,0:T(1,128)S(1)}, s32[1,32]{1,0:T(1,128)}, u32[]{:S(2)}) copy-start(s32[1,32]{1,0:T(1,128)} %param.13) | copy-start | bytes 388
  7.2 32.1 %all-gather.19.cloned.1.call-start = ((), (), s32[]{:S(2)}) async-start(), calls=%async_computation.7 | async-start | bytes 1310720 | tf_op jit(solution)/shard_map/all_gather | solution.py:76
  7.9 151.1 %all-gather.11.cloned.1.call-start = ((), (), s32[]{:S(2)}) async-start(), calls=%async_computation.2 | async-start | bytes 4259840 | tf_op jit(solution)/shard_map/all_gather | solution.py:70
  8.7 238.3 %all-gather.17.cloned.1.call-start = ((), (), s32[]{:S(2)}) async-start(), calls=%async_computation.6 | async-start | bytes 4325376 | tf_op jit(solution)/shard_map/all_gather | solution.py:36
  9.4 324.2 %all-gather.15.cloned.1.call-start = ((), (), s32[]{:S(2)}) async-start(), calls=%async_computation.5 | async-start | bytes 4325376 | tf_op jit(solution)/shard_map/all_gather | solution.py:35
  11.1 409.5 %all-gather.21.cloned.1.call-start = ((), (), s32[]{:S(2)}) async-start(), calls=%async_computation.8 | async-start | bytes 4325376 | tf_op jit(solution)/shard_map/all_gather | solution.py:127
  12.9 494.6 %all-gather.13.cloned.1.call-start = ((), (), s32[]{:S(2)}) async-start(), calls=%async_computation.4 | async-start | bytes 4325376 | tf_op jit(solution)/shard_map/all_gather | solution.py:128
  163.0 368.6 %reduce-scatter.5.cloned.1.call-start = ((), (), s32[]{:S(2)}) async-start(), calls=%async_computation.3 | async-start | bytes 1310720 | tf_op jit(solution)/shard_map/reduce_scatter | solution.py:73
  163.7 169.9 %copy-start.3 = (bf16[1,128,512]{1,2,0:T(8,128)(2,1)S(1)}, bf16[1,128,512]{1,2,0:T(8,128)(2,1)}, u32[]{:S(2)}) copy-start(bf16[1,128,512]{1,2,0:T(8,128)(2,1)} %copy.106) | copy-start | bytes 393220
  337.9 3.2 copy-start
  341.1 2.5 copy-start.4
  343.7 7.3 copy-start.1
  351.1 2.6 copy-start.2
  353.6 455.5 %reduce-scatter.7.cloned.1.call-start = ((), (), s32[]{:S(2)}) async-start(), calls=%async_computation.9 | async-start | bytes 8519680
  367.1 0.9 copy-start.5
  367.2 1.0 copy-start.6
Sparse Core Ops, SparseCore 0:
  9.8 29.3 all-gather.18
  41.1 117.9 all-gather.10
  161.8 85.0 all-gather.16
  249.9 83.5 all-gather.14
  336.6 83.9 all-gather.20
  423.8 83.6 all-gather.12
  510.6 20.9 reduce-scatter.4
  534.8 274.1 reduce-scatter.6
where the time goes:
time: 823 us; the launch traced here: 816 us
  waiting for transfers between devices  600 us (73%)
  blocking collectives  79.3 us (10%)
  local copies, waits for them, and re-layouts  56.7 us (7%)
  matrix products  52.3 us (6%)
  between operations  14.3 us (2%)
    unnamed x9, waiting for transfers between devices  280 us
    all_gather x1, waiting for transfers between devices, on_device(): portion = lax.all_gather(out_weight, ('dp', 'ctx'), axis=0, tiled=True)  120 us
    all_gather x1, waiting for transfers between devices, on_device(): value_piece = lax.all_gather(own_values, 'ctx', axis=0, tiled=True)  83.2 us
    all_gather x1, waiting for transfers between devices, on_device(): key_piece = lax.all_gather(own_keys, 'ctx', axis=0, tiled=True)  80.2 us
    all_gather x1, blocking collectives, on_device(): lax.all_gather(log_total, 'ctx', axis=0, tiled=True)  39.7 us
    all_gather x1, blocking collectives, on_device(): lax.all_gather(row_delta, 'ctx', axis=0, tiled=True)  39.6 us
    all_gather x1, waiting for transfers between devices, on_device(): grad_full = lax.all_gather(out_grad[0], 'mp', axis=1, tiled=True)  26.3 us
    dynamic_slice x32, local copies, waits for them, and re-layouts, on_device(): lax.scan(query_step, jnp.zeros((tok_rows, head_count, HD), jnp.float32),...  18.3 us
  transfers between devices with their start and end apart: 8, of which 8 were waited for; matrix products, arithmetic and copies ran while one was open for 14% of the time, Pallas kernels for 0%

commit v1 on v0

v1 whole, which is shorter than its diff:
```python
import functools

import jax
import jax.numpy as jnp
from jax import lax
from jax.experimental import pallas as pl
from jax.experimental.pallas import tpu as pltpu
from jax.sharding import PartitionSpec as P

HD = 128
MASKED = -1e30
MESH = pl.DeviceIdType.MESH
BF = jnp.bfloat16
F32 = jnp.float32
PHASES = ((-1, 1), (-2, 2), (-3, 3), (4,))


class Place:
    def __init__(self):
        self.dp = lax.axis_index("dp")
        self.ctx = lax.axis_index("ctx")
        self.mp = lax.axis_index("mp")
        self.z = self.ctx // 4
        self.j = self.ctx % 4
        self.yhi = self.j // 2
        self.core = self.j % 2
        self.y = self.yhi * 2 + self.dp

    def plane(self, off):
        return (self.z + 8 + off) % 8

    def yblock(self, off):
        y = (self.y + 4 + off) % 4
        return y % 2, y // 2

    def at_z(self, off):
        return {"ctx": self.plane(off) * 4 + self.j}

    def at_y(self, off):
        dp, yhi = self.yblock(off)
        return {"dp": dp, "ctx": self.z * 4 + yhi * 2 + self.core}

    def at_x(self, off):
        return {"mp": (self.mp + 4 + off) % 4}

    def at_j(self, off):
        return {"ctx": self.z * 4 + (self.j + 4 + off) % 4}

    def sibling(self):
        return {"ctx": self.ctx + 1 - 2 * self.core}


def greet(devices):
    barrier = pltpu.get_barrier_semaphore()
    for device in devices:
        pl.semaphore_signal(barrier, inc=1, device_id=device, device_id_type=MESH)
    pl.semaphore_wait(barrier, len(devices))


class Links:
    def __init__(self, send_sems, recv_sems):
        self.send_sems, self.recv_sems = send_sems, recv_sems
        self.slots = {}
        self.sent = []

    def slot(self, name):
        return self.slots.setdefault(name, len(self.slots))

    def copy(self, name, src, dst, device):
        i = self.slot(name)
        return pltpu.make_async_remote_copy(
            src_ref=src, dst_ref=dst, send_sem=self.send_sems.at[i],
            recv_sem=self.recv_sems.at[i], device_id=device, device_id_type=MESH)

    def send(self, name, src, dst, device):
        copy = self.copy(name, src, dst, device)
        copy.start()
        self.sent.append(copy)

    def wait(self, name, dst, device):
        self.copy(name, dst, dst, device).wait_recv()

    def drain(self):
        for copy in self.sent:
            copy.wait_send()


def gather_kernel(q, k, v, w, og, qh, kv, wf, ogf, send_sems, recv_sems, local_sems):
    at = Place()
    z, j, core = at.z, at.j, at.core
    greet([at.at_j(1), at.at_j(2), at.at_j(3), at.at_z(1), at.at_z(-1),
           at.at_y(1), at.at_y(-1), at.at_x(1), at.at_x(-1)])
    links = Links(send_sems, recv_sems)

    def head(ref, off):
        return ref.at[:, pl.ds(pl.multiple_of((j + 4 + off) % 4 * HD, HD), HD)]

    def wblock(zoff, yoff, half=None):
        dp, yhi = at.yblock(yoff)
        ref = wf.at[dp, at.plane(zoff), yhi, core]
        return ref if half is None else ref.at[pl.ds(half * 32, 32)]

    own = [
        pltpu.make_async_copy(head(k, 0), kv.at[0, z, j], local_sems.at[0]),
        pltpu.make_async_copy(head(v, 0), kv.at[1, z, j], local_sems.at[1]),
        pltpu.make_async_copy(w, wblock(0, 0), local_sems.at[2]),
        pltpu.make_async_copy(head(q, 0), qh.at[j], local_sems.at[3]),
        pltpu.make_async_copy(og, ogf.at[at.mp], local_sems.at[4]),
    ]
    for copy in own:
        copy.start()
    for a, ref in ((0, k), (1, v)):
        for t in (1, 2, 3):
            links.send(("kv", a, t), head(ref, t), kv.at[a, z, j], at.at_j(t))
    for d in (1, -1):
        links.send(("wz", d, 0), w, wblock(0, 0), at.at_z(d))
        links.send(("wy", 0, d), w, wblock(0, 0), at.at_y(d))
    for d in (1, -1):
        links.send(("og", d, 0), og, ogf.at[at.mp], at.at_x(d))
    for t in (1, 2, 3):
        links.send(("q", t), head(q, t), qh.at[j], at.at_j(t))
    own[0].wait()
    own[1].wait()
    for a in (0, 1):
        for t in (1, 2, 3):
            links.wait(("kv", a, t), kv.at[a, z, (j + 4 - t) % 4], at.at_j(t))
        for d in (1, -1):
            links.send(("z", a, d, 0), kv.at[a, z], kv.at[a, z], at.at_z(d))
    own[2].wait()

    def forward_y(off):
        for d in (1, -1):
            links.wait(("wy", off, d), wblock(off, -d), at.at_y(d))
            half = (1 - d) // 2
            links.send(("wyh", off, d), wblock(off, -d, half), wblock(off, -d, half), at.at_y(d))

    def to_sibling(off):
        for d in (1, -1):
            half = (1 - d) // 2
            links.wait(("wyh", off, d), wblock(off, 2, half), at.at_y(d))
        for dp in (0, 1):
            ref = wf.at[dp, at.plane(off), :, core]
            links.send(("sib", off, dp), ref, ref, at.sibling())

    done = (0,)
    before = ()
    for s in range(4):
        for d in (1, -1):
            if s < 3:
                links.wait(("wz", d, s), wblock(-d * (1 + s), 0), at.at_z(d))
            else:
                half = (1 - d) // 2
                links.wait(("wz", d, s), wblock(4, 0, half), at.at_z(d))
            if s < 2:
                links.send(("wz", d, s + 1), wblock(-d * (1 + s), 0), wblock(-d * (1 + s), 0), at.at_z(d))
            elif s == 2:
                half = (1 - d) // 2
                links.send(("wz", d, 3), wblock(-d * 3, 0, half), wblock(-d * 3, 0, half), at.at_z(d))
        for off in PHASES[s]:
            for d in (1, -1):
                links.send(("wy", off, d), wblock(off, 0), wblock(off, 0), at.at_y(d))
        for off in done:
            forward_y(off)
        if s == 0:
            for d in (1, -1):
                links.wait(("og", d, 0), ogf.at[(at.mp + 4 - d) % 4], at.at_x(d))
                half = ogf.at[(at.mp + 4 - d) % 4, pl.ds((1 - d) // 2 * 64, 64)]
                links.send(("og", d, 1), half, half, at.at_x(d))
        for a in (0, 1):
            for d in (1, -1):
                if s == 3 and a != (1 - d) // 2:
                    continue
                chunk = kv.at[a, at.plane(-d * (1 + s))]
                links.wait(("z", a, d, s), chunk, at.at_z(d))
                if s < 2 or (s == 2 and a == (1 - d) // 2):
                    links.send(("z", a, d, s + 1), chunk, chunk, at.at_z(d))
        for off in before:
            to_sibling(off)
        before = done
        done = PHASES[s]
    for off in done:
        forward_y(off)
    for off in before + done:
        to_sibling(off)
    for d in (1, -1):
        half = ogf.at[(at.mp + 2) % 4, pl.ds((1 - d) // 2 * 64, 64)]
        links.wait(("og", d, 1), half, at.at_x(d))
    for t in (1, 2, 3):
        links.wait(("q", t), qh.at[(j + 4 - t) % 4], at.at_j(t))
    for off in (0, -1, 1, -2, 2, -3, 3, 4):
        for dp in (0, 1):
            ref = wf.at[dp, at.plane(off), :, 1 - core]
            links.wait(("sib", off, dp), ref, at.sibling())
    own[3].wait()
    own[4].wait()
    links.drain()
    assert len(links.slots) <= 96, len(links.slots)


def any_spec(n):
    return [pl.BlockSpec(memory_space=pl.ANY)] * n


def gather(q, k, v, w, og):
    return pl.pallas_call(
        gather_kernel,
        out_shape=(
            jax.ShapeDtypeStruct((4, 128, HD), BF),
            jax.ShapeDtypeStruct((2, 8, 4, 128, HD), BF),
            jax.ShapeDtypeStruct((2, 8, 2, 2, 64, 512), BF),
            jax.ShapeDtypeStruct((4, 128, 1024), BF),
        ),
        in_specs=any_spec(5),
        out_specs=tuple(any_spec(4)),
        scratch_shapes=[
            pltpu.SemaphoreType.DMA((96,)),
            pltpu.SemaphoreType.DMA((96,)),
            pltpu.SemaphoreType.DMA((5,)),
        ],
        compiler_params=pltpu.CompilerParams(collective_id=0, has_side_effects=True),
        name="gather",
    )(q, k, v, w, og)

ORDER = (4, 3, -3, 2, -2, 1, -1, 0)
GROUPS = ((4,), (3, -3), (2, -2), (1, -1), (0,))
LOG2E = 1.4426950408889634
SCALE2 = HD ** -0.5 * LOG2E
NT = (((1,), (1,)), ((), ()))
TN = (((0,), (0,)), ((), ()))


def dot(a, b, dims=(((1,), (0,)), ((), ()))):
    return lax.dot_general(a, b, dims, preferred_element_type=F32)


def swap_kernel(gh, att, doh, att_tok, send_sems, recv_sems, local_sems):
    at = Place()
    j = at.j
    greet([at.at_j(1), at.at_j(2), at.at_j(3)])
    links = Links(send_sems, recv_sems)

    def head(ref, off):
        return ref.at[:, pl.ds(pl.multiple_of((j + 4 + off) % 4 * HD, HD), HD)]

    own = [
        pltpu.make_async_copy(head(gh, 0), doh.at[j], local_sems.at[0]),
        pltpu.make_async_copy(att.at[j], head(att_tok, 0), local_sems.at[1]),
    ]
    for t in (1, 2, 3):
        links.send(("g", t), head(gh, t), doh.at[j], at.at_j(t))
        links.send(("a", t), att.at[(j + t) % 4], head(att_tok, 0), at.at_j(t))
    for copy in own:
        copy.start()
    for t in (1, 2, 3):
        links.wait(("g", t), doh.at[(j + 4 - t) % 4], at.at_j(t))
        links.wait(("a", t), head(att_tok, -t), at.at_j(t))
    for copy in own:
        copy.wait()
    links.drain()


def swap(gh, att):
    return pl.pallas_call(
        swap_kernel,
        out_shape=(
            jax.ShapeDtypeStruct((4, 128, HD), BF),
            jax.ShapeDtypeStruct((128, 512), BF),
        ),
        in_specs=any_spec(2),
        out_specs=tuple(any_spec(2)),
        scratch_shapes=[
            pltpu.SemaphoreType.DMA((6,)),
            pltpu.SemaphoreType.DMA((6,)),
            pltpu.SemaphoreType.DMA((2,)),
        ],
        compiler_params=pltpu.CompilerParams(collective_id=1, has_side_effects=True),
        name="swap",
    )(gh, att)


def half_of(d):
    return (1 - d) // 2


def scatter_kernel(dq_h, dkv, px, wgp, dq, dk, dv, proj, wg,
                   zr, zs, zfin, xr0, xs, xr1, sibr, wsum, yr0, yr1, wy, wzr, wzs,
                   send_sems, recv_sems, local_sems):
    at = Place()
    z, j, core = at.z, at.j, at.core
    greet([at.at_j(1), at.at_j(2), at.at_j(3), at.at_z(1), at.at_z(-1),
           at.at_y(1), at.at_y(-1), at.at_x(1), at.at_x(-1)])
    links = Links(send_sems, recv_sems)

    def head(ref, off):
        return ref.at[:, pl.ds(pl.multiple_of((j + 4 + off) % 4 * HD, HD), HD)]

    def plus(*terms):
        total = terms[0].astype(F32)
        for term in terms[1:]:
            total = total + term.astype(F32)
        return total

    own = [pltpu.make_async_copy(dq_h.at[j], head(dq, 0), local_sems.at[0])]

    def zsend(s, only=None):
        for i, d in ((0, 1), (1, -1)):
            for a in (0, 1):
                if s == 0 and a != i:
                    continue
                if only is not None and only != (s == 1 and a != i):
                    continue
                p = at.plane(d * (4 - s))
                if s == 0 or (s == 1 and a != i):
                    src = dkv.at[a, p]
                else:
                    links.wait(("z", a, d, s - 1), zr.at[a, i, s - 1], at.at_z(d))
                    zs[a, i, s - 1] = plus(dkv[a, p], zr[a, i, s - 1]).astype(BF)
                    src = zs.at[a, i, s - 1]
                links.send(("z", a, d, s), src, zr.at[a, i, s], at.at_z(d))

    def zfinal():
        for a, out in ((0, dk), (1, dv)):
            for i, d in ((0, 1), (1, -1)):
                links.wait(("z", a, d, 3), zr.at[a, i, 3], at.at_z(d))
            zfin[a] = plus(dkv[a, z], zr[a, 0, 3], zr[a, 1, 3]).astype(BF)
            for t in (1, 2, 3):
                links.send(("kv", a, t), zfin.at[a, (j + t) % 4], head(out, 0), at.at_j(t))
            copy = pltpu.make_async_copy(zfin.at[a, j], head(out, 0), local_sems.at[1 + a])
            copy.start()
            own.append(copy)

    def xfirst():
        for i, d in ((0, 1), (1, -1)):
            links.send(("x", d, 0), px.at[(at.mp + 2) % 4, pl.ds(i * 64, 64)], xr0.at[i], at.at_x(d))

    def xsecond():
        for i, d in ((0, 1), (1, -1)):
            chunk = (at.mp + 4 + d) % 4
            links.wait(("x", d, 0), xr0.at[i], at.at_x(d))
            xs[i, pl.ds(i * 64, 64)] = plus(px[chunk, pl.ds(i * 64, 64)], xr0[i]).astype(BF)
            xs[i, pl.ds(64 - i * 64, 64)] = px[chunk, pl.ds(64 - i * 64, 64)]
            links.send(("x", d, 1), xs.at[i], xr1.at[i], at.at_x(d))

    def xfinal():
        for i, d in ((0, 1), (1, -1)):
            links.wait(("x", d, 1), xr1.at[i], at.at_x(d))
        proj[...] = plus(px[at.mp], xr1[0], xr1[1]).astype(BF)

    def to_sibling(off):
        for dp in (0, 1):
            p = at.plane(off)
            links.send(("sib", off, dp), wgp.at[dp, p, :, 1 - core], sibr.at[dp, p], at.sibling())

    def yfirst(off):
        p = at.plane(off)
        for dp in (0, 1):
            links.wait(("sib", off, dp), sibr.at[dp, p], at.sibling())
        for dp in (0, 1):
            for yhi in (0, 1):
                wsum[dp, p, yhi] = plus(wgp[dp, p, yhi, core], sibr[dp, p, yhi]).astype(BF)
        dp, yhi = at.yblock(2)
        for i, d in ((0, 1), (1, -1)):
            links.send(("y", off, d, 0), wsum.at[dp, p, yhi, pl.ds(i * 32, 32)], yr0.at[p, i], at.at_y(d))

    def ysecond(off):
        p = at.plane(off)
        for i, d in ((0, 1), (1, -1)):
            dp, yhi = at.yblock(d)
            links.wait(("y", off, d, 0), yr0.at[p, i], at.at_y(d))
            rows = pl.ds(i * 32, 32)
            wsum[dp, p, yhi, rows] = plus(wsum[dp, p, yhi, rows], yr0[p, i]).astype(BF)
            links.send(("y", off, d, 1), wsum.at[dp, p, yhi], yr1.at[p, i], at.at_y(d))

    def yfinal(off):
        p = at.plane(off)
        for i, d in ((0, 1), (1, -1)):
            links.wait(("y", off, d, 1), yr1.at[p, i], at.at_y(d))
        total = plus(wsum[at.dp, p, at.yhi], yr1[p, 0], yr1[p, 1])
        if off == 0:
            for i, d in ((0, 1), (1, -1)):
                links.wait(("w", d, 3), wzr.at[i, 3], at.at_z(d))
            wg[...] = plus(total, wzr[0, 3], wzr[1, 3])
            return
        if off == 4:
            wy[...] = total.astype(BF)
            for i, d in ((0, 1), (1, -1)):
                rows = pl.ds(i * 32, 32)
                links.send(("w", d, 0), wy.at[rows], wzr.at[i, 0, rows], at.at_z(d))
            return
        d = 1 if off > 0 else -1
        i = half_of(d)
        s = 4 - abs(off)
        if s == 1:
            rows = pl.ds(i * 32, 32)
            rest = pl.ds(32 - i * 32, 32)
            links.wait(("w", d, 0), wzr.at[i, 0, rows], at.at_z(d))
            wzs[i, 0] = total.astype(BF)
            wzs[i, 0, rows] = plus(total[i * 32:i * 32 + 32], wzr[i, 0, rows]).astype(BF)
        else:
            links.wait(("w", d, s - 1), wzr.at[i, s - 1], at.at_z(d))
            wzs[i, s - 1] = plus(total, wzr[i, s - 1]).astype(BF)
        links.send(("w", d, s), wzs.at[i, s - 1], wzr.at[i, s], at.at_z(d))

    def each(step, group):
        for off in GROUPS[group]:
            step(off)

    zsend(0)
    zsend(1, True)
    to_sibling(4)
    xfirst()
    for off in ORDER[1:]:
        to_sibling(off)
    for t in (1, 2, 3):
        links.send(("q", t), dq_h.at[(j + t) % 4], head(dq, 0), at.at_j(t))
    own[0].start()
    each(yfirst, 0)
    each(yfirst, 1)
    each(ysecond, 0)
    zsend(1, False)
    xsecond()
    each(yfirst, 2)
    each(ysecond, 1)
    each(yfinal, 0)
    zsend(2)
    each(yfirst, 3)
    each(ysecond, 2)
    each(yfinal, 1)
    zsend(3)
    xfinal()
    each(yfirst, 4)
    each(ysecond, 3)
    each(yfinal, 2)
    zfinal()
    each(ysecond, 4)
    each(yfinal, 3)
    each(yfinal, 4)
    for t in (1, 2, 3):
        links.wait(("q", t), head(dq, -t), at.at_j(t))
        links.wait(("kv", 0, t), head(dk, -t), at.at_j(t))
        links.wait(("kv", 1, t), head(dv, -t), at.at_j(t))
    for copy in own:
        copy.wait()
    links.drain()
    assert len(links.slots) <= 96, len(links.slots)


def vmem(n):
    return [pl.BlockSpec(memory_space=pltpu.VMEM)] * n


def scatter(dq_h, dkv, px, wgp):
    return pl.pallas_call(
        scatter_kernel,
        out_shape=(
            jax.ShapeDtypeStruct((128, 512), BF),
            jax.ShapeDtypeStruct((128, 512), BF),
            jax.ShapeDtypeStruct((128, 512), BF),
            jax.ShapeDtypeStruct((128, 1024), BF),
            jax.ShapeDtypeStruct((64, 512), F32),
        ),
        in_specs=vmem(4),
        out_specs=tuple(vmem(5)),
        scratch_shapes=[
            pltpu.VMEM((2, 2, 4, 4, 128, HD), BF),
            pltpu.VMEM((2, 2, 3, 4, 128, HD), BF),
            pltpu.VMEM((2, 4, 128, HD), BF),
            pltpu.VMEM((2, 64, 1024), BF),
            pltpu.VMEM((2, 128, 1024), BF),
            pltpu.VMEM((2, 128, 1024), BF),
            pltpu.VMEM((2, 8, 2, 64, 512), BF),
            pltpu.VMEM((2, 8, 2, 64, 512), BF),
            pltpu.VMEM((8, 2, 32, 512), BF),
            pltpu.VMEM((8, 2, 64, 512), BF),
            pltpu.VMEM((64, 512), BF),
            pltpu.VMEM((2, 4, 64, 512), BF),
            pltpu.VMEM((2, 3, 64, 512), BF),
            pltpu.SemaphoreType.DMA((96,)),
            pltpu.SemaphoreType.DMA((96,)),
            pltpu.SemaphoreType.DMA((3,)),
        ],
        compiler_params=pltpu.CompilerParams(
            collective_id=2, has_side_effects=True, vmem_limit_bytes=40 << 20),
        name="scatter",
    )(dq_h, dkv, px, wgp)


def forward_kernel(offsets, posq, qh, kv, wf, ogf, gh, att, lse, scores, top):
    total = dot(ogf[0], wf[pl.ds(0, 1024)])
    for x in (1, 2, 3):
        total += dot(ogf[x], wf[pl.ds(x * 1024, 1024)])
    gh[...] = total.astype(BF)
    q = qh[...]
    row_in = lax.broadcasted_iota(jnp.int32, (128, 512), 0)
    top[...] = jnp.full((8, 512), MASKED, F32)

    @pl.loop(0, 32)
    def _(b):
        rows = pl.ds(pl.multiple_of(b * 128, 128), 128)
        s = dot(kv[0, rows], q, NT) * SCALE2
        s = jnp.where(row_in <= posq[...] - offsets[0, b] * 128, s, MASKED)
        scores[rows] = s
        top[...] = jnp.maximum(top[...], jnp.max(s.reshape(16, 8, 512), axis=0))

    m = jnp.max(top[...], axis=0, keepdims=True)

    def step(b, carry):
        acc, total = carry
        rows = pl.ds(pl.multiple_of(b * 256, 256), 256)
        p = jnp.exp2(scores[rows] - m)
        total = total + jnp.sum(p.reshape(32, 8, 512), axis=0)
        acc = acc + dot(kv[1, rows], p.astype(BF), TN)
        return acc, total

    acc, total = lax.fori_loop(
        0, 16, step, (jnp.zeros((HD, 512), F32), jnp.zeros((8, 512), F32)))
    total = jnp.sum(total, axis=0, keepdims=True)
    att[...] = (acc / total).T.astype(BF)
    lse[...] = m + jnp.log2(total)


def forward(offsets, posq, qh, kv, wf, ogf):
    return pl.pallas_call(
        forward_kernel,
        out_shape=(
            jax.ShapeDtypeStruct((128, 512), BF),
            jax.ShapeDtypeStruct((512, HD), BF),
            jax.ShapeDtypeStruct((1, 512), F32),
        ),
        in_specs=[pl.BlockSpec(memory_space=pltpu.SMEM)] + vmem(5),
        out_specs=tuple(vmem(3)),
        scratch_shapes=[pltpu.VMEM((4096, 512), F32), pltpu.VMEM((8, 512), F32)],
        compiler_params=pltpu.CompilerParams(vmem_limit_bytes=40 << 20),
        name="forward",
    )(offsets, posq, qh, kv, wf, ogf)


def backward_kernel(offsets, posq, qh, kv, wf, ogf, doh, att_tok, att, lse,
                    dq, dkv, px, wgp):
    a = att_tok[...]
    for x in range(4):
        rows = pl.ds(x * 1024, 1024)
        px[x] = dot(a, wf[rows], NT).astype(BF)
        wgp[rows] = dot(ogf[x], a, TN).astype(BF)
    q = qh[...]
    do = doh[...]
    delta = jnp.sum((do.astype(F32) * att[...].astype(F32)).T, axis=0, keepdims=True)
    row_in = lax.broadcasted_iota(jnp.int32, (128, 512), 0)

    def step(b, acc):
        rows = pl.ds(pl.multiple_of(b * 128, 128), 128)
        k, v = kv[0, rows], kv[1, rows]
        s = dot(k, q, NT) * SCALE2
        p = jnp.where(row_in <= posq[...] - offsets[0, b] * 128, jnp.exp2(s - lse[...]), 0.0)
        ds = (p * (dot(v, do, NT) - delta)).astype(BF)
        dkv[1, rows] = dot(p.astype(BF), do).astype(BF)
        dkv[0, rows] = (dot(ds, q) * HD ** -0.5).astype(BF)
        return acc + dot(k, ds, TN)

    acc = lax.fori_loop(0, 32, step, jnp.zeros((HD, 512), F32))
    dq[...] = (acc * HD ** -0.5).T.astype(BF)


def backward(offsets, posq, qh, kv, wf, ogf, doh, att_tok, att, lse):
    return pl.pallas_call(
        backward_kernel,
        out_shape=(
            jax.ShapeDtypeStruct((512, HD), BF),
            jax.ShapeDtypeStruct((2, 4096, HD), BF),
            jax.ShapeDtypeStruct((4, 128, 1024), BF),
            jax.ShapeDtypeStruct((4096, 512), BF),
        ),
        in_specs=[pl.BlockSpec(memory_space=pltpu.SMEM)] + vmem(9),
        out_specs=tuple(vmem(4)),
        compiler_params=pltpu.CompilerParams(vmem_limit_bytes=40 << 20),
        name="backward",
    )(offsets, posq, qh, kv, wf, ogf, doh, att_tok, att, lse)


def on_device(queries, key_rows, value_rows, out_weight, out_grad, block_offsets):
    qh, kv, wf, ogf = gather(queries[0], key_rows[0], value_rows[0], out_weight, out_grad[0])
    plane = lax.axis_index("ctx") // 4
    mine = lax.dynamic_slice(block_offsets, (0, plane * 4), (1, 4))
    posq = (mine.reshape(4, 1) * 128 + jnp.arange(128, dtype=jnp.int32)[None, :]).reshape(1, 512)
    qh = qh.reshape(512, HD)
    kv = kv.reshape(2, 4096, HD)
    wf = wf.reshape(4096, 512)
    gh, att, lse = forward(block_offsets, posq, qh, kv, wf, ogf)
    doh, att_tok = swap(gh, att.reshape(4, 128, HD))
    dq_h, dkv, px, wgp = backward(
        block_offsets, posq, qh, kv, wf, ogf, doh.reshape(512, HD), att_tok, att, lse)
    dq, dk, dv, proj, wg = scatter(
        dq_h.reshape(4, 128, HD), dkv.reshape(2, 8, 4, 128, HD), px,
        wgp.reshape(2, 8, 2, 2, 64, 512))
    return proj[None], dq[None], dk[None], dv[None], wg


def solution(mesh):
    tokens = P("dp", "ctx", "mp")
    features = P(("dp", "ctx"), "mp")
    return jax.shard_map(
        on_device,
        mesh=mesh,
        in_specs=(tokens, tokens, tokens, features, tokens, P("dp", None)),
        out_specs=(tokens, tokens, tokens, tokens, features),
        check_vma=False,
    )
```

time: 823 us -> 137 us (0.17)
  waiting for transfers between devices: 600 us -> 0 us
  Pallas kernels: 0 us -> 121 us
  blocking collectives: 79.3 us -> 0 us
  matrix products: 52.3 us -> 0 us
  local copies, waits for them, and re-layouts: 56.7 us -> 13.9 us
  between operations: 14.3 us -> 0.76 us
    all_gather x6 -> x0, waiting for transfers between devices: 319 us -> none  [the longest x1 120 us: on_device(): portion = lax.all_gather(out_weight, ('dp', 'ctx'), axis=0, tiled=True)]
    unnamed x9 -> x0, waiting for transfers between devices: 280 us -> none
    pallas_call x0 -> x5, Pallas kernels: none -> 121 us  [the longest x1 48.8 us: gather(): pl.pallas_call(gather_kernel, out_shape=(jax.ShapeDtypeStruct((4, 128, HD...]
    all_gather x2 -> x0, blocking collectives: 79.3 us -> none  [the longest x1 39.7 us: on_device(): lax.all_gather(log_total, 'ctx', axis=0, tiled=True)]
    dot_general x24 -> x0, matrix products: 52.3 us -> none  [the longest x1 8.05 us: on_device(): jnp.einsum('hnk,nhd->khd', score_grad, query_part, preferred_element_type...]
    dynamic_slice x32 -> x0, local copies, waits for them, and re-layouts: 18.3 us -> none  [on_device(): lax.scan(query_step, jnp.zeros((tok_rows, head_count, HD), jnp.float32),...]
    all_gather x2 -> x0, local copies, waits for them, and re-layouts: 12.9 us -> none  [the longest x1 6.48 us: on_device(): key_piece = lax.all_gather(own_keys, 'ctx', axis=0, tiled=True)]
    unnamed x23 -> x33, local copies, waits for them, and re-layouts: 18.2 us -> 13.9 us
  transfers between devices with their start and end apart: 8 -> 0, of which waited for: 8 -> 0; matrix products, arithmetic and copies ran while one was open for 14% -> 0% of each run, Pallas kernels for 0% -> 0%
where the time goes in v1:
time: 137 us; the launch traced here: 136 us
  Pallas kernels  121 us (88%)
  local copies, waits for them, and re-layouts  13.9 us (10%)
    pallas_call x1, Pallas kernels, gather(): pl.pallas_call(gather_kernel, out_shape=(jax.ShapeDtypeStruct((4, 128, HD...  48.8 us
    pallas_call x1, Pallas kernels, scatter(): pl.pallas_call(scatter_kernel, out_shape=(jax.ShapeDtypeStruct((128, 512)...  34.3 us
    pallas_call x1, Pallas kernels, backward(): pl.pallas_call(backward_kernel, out_shape=(jax.ShapeDtypeStruct((512, HD)...  18.8 us
    unnamed x33, local copies, waits for them, and re-layouts  13.9 us
    pallas_call x1, Pallas kernels, forward(): pl.pallas_call(forward_kernel, out_shape=(jax.ShapeDtypeStruct((128, 512)...  11.8 us
    pallas_call x1, Pallas kernels, swap(): pl.pallas_call(swap_kernel, out_shape=(jax.ShapeDtypeStruct((4, 128, HD),...  7.21 us

profile of v1, /device:TPU:1, one launch (start us, length us, event | category | flops | bytes accessed | tf_op | source)
XLA Modules:
  0.0 136.4 jit_solution(1004777591236043588)
XLA Ops:
  0.6 0.7 multiply_bitcast_fusion
  1.4 0.1 iota_add_fusion
  1.5 0.0 copy-start.13
  1.5 48.8 %gather.1 = (bf16[4,128,128]{2,1,0:T(8,128)(2,1)}, bf16[2,8,4,128,128]{4,3,2,1,0:T(8,128)(2,1)}, bf16[2,8,2,2,64,512]{5,4,3,2,1,0:T(8,128)(2,1)}, bf16[4,128,1024]{2,1,0:T(8,128)(2,1)}) custom-call(bf16[128,512]{1,0:T(8,128)(2,1)} %bitcast.37, bf16[128,512]{1,0:T(8,128)(2,1)} %bitcast.38, bf16[128,512]{1,0:T(8,128)(2,1)} %bitcast.39, bf16[64,512]{1,0:T(8,128)(2,1)} %w.1, ...), custom_call_target="tpu_custom_call" | custom-call | tf_op jit(solution)/shard_map/gather/pallas_call | solution.py:205
  50.3 0.0 copy-start
  50.3 2.2 %copy-done = bf16[2,8,2,2,64,512]{5,4,3,2,1,0:T(8,128)(2,1)S(1)} copy-done((bf16[2,8,2,2,64,512]{5,4,3,2,1,0:T(8,128)(2,1)S(1)}, bf16[2,8,2,2,64,512]{5,4,3,2,1,0:T(8,128)(2,1)}, u32[]{:S(2)}) %copy-start) | copy-done | bytes 4194328
  52.5 0.0 copy-start.1
  52.5 1.6 %copy-done.1 = bf16[2,8,4,128,128]{4,3,2,1,0:T(8,128)(2,1)S(1)} copy-done((bf16[2,8,4,128,128]{4,3,2,1,0:T(8,128)(2,1)S(1)}, bf16[2,8,4,128,128]{4,3,2,1,0:T(8,128)(2,1)}, u32[]{:S(2)}) %copy-start.1) | copy-done | bytes 2097176
  54.0 0.0 copy-start.3
  54.1 1.2 copy-done.3
  55.3 0.9 copy-done.5
  56.2 0.7 copy-done.12
  56.8 11.8 %forward.1 = (bf16[128,512]{1,0:T(8,128)(2,1)S(1)}, bf16[512,128]{1,0:T(8,128)(2,1)S(1)}, f32[1,512]{1,0:T(1,128)S(1)}) custom-call(s32[1,32]{1,0:T(1,128)S(1)} %copy-done.12, s32[1,512]{1,0:T(1,128)S(1)} %bitcast.34, bf16[512,128]{1,0:T(8,128)(2,1)S(1)} %bitcast.25, bf16[2,4096,128]{2,1,0:T(8,128)(2,1)S(1)} %bitcast.21, bf16[4096,512]{1,0:T(8,128)(2,1)S(1)} %bitcast.20, ...), custom_call_target="tpu_custom_call" | custom-call | tf_op jit(solution)/shard_map/forward/pallas_call | solution.py:523
  68.7 0.0 copy-start.7
  68.7 0.6 copy-done.7
  69.4 0.7 copy-done.11
  70.0 7.2 %swap.1 = (bf16[4,128,128]{2,1,0:T(8,128)(2,1)}, bf16[128,512]{1,0:T(8,128)(2,1)}) custom-call(bf16[128,512]{1,0:T(8,128)(2,1)} %copy-done.11, bf16[4,128,128]{2,1,0:T(8,128)(2,1)} %bitcast.27), custom_call_target="tpu_custom_call" | custom-call | tf_op jit(solution)/shard_map/swap/pallas_call | solution.py:263
  77.2 0.0 copy-done.13
  77.2 0.0 copy-done.2
  77.3 0.0 copy-done.4
  77.3 0.0 copy-done.6
  77.3 0.0 copy-start.8
  77.3 0.9 copy-done.8
  78.2 0.9 copy-done.9
  79.1 0.9 copy-done.10
  80.0 18.8 %backward.1 = (bf16[512,128]{1,0:T(8,128)(2,1)S(1)}, bf16[2,4096,128]{2,1,0:T(8,128)(2,1)S(1)}, bf16[4,128,1024]{2,1,0:T(8,128)(2,1)S(1)}, bf16[4096,512]{1,0:T(8,128)(2,1)S(1)}) custom-call(s32[1,32]{1,0:T(1,128)S(1)} %copy-done.13, s32[1,512]{1,0:T(1,128)S(1)} %bitcast.35, bf16[512,128]{1,0:T(8,128)(2,1)S(1)} %bitcast.26, ...), custom_call_target="tpu_custom_call" | custom-call | tf_op jit(solution)/shard_map/backward/pallas_call | solution.py:565
  98.8 34.3 %scatter.1 = (bf16[128,512]{1,0:T(8,128)(2,1)S(1)}, bf16[128,512]{1,0:T(8,128)(2,1)S(1)}, bf16[128,512]{1,0:T(8,128)(2,1)S(1)}, bf16[128,1024]{1,0:T(8,128)(2,1)S(1)}, f32[64,512]{1,0:T(8,128)S(1)}) custom-call(bf16[4,128,128]{2,1,0:T(8,128)(2,1)S(1)} %bitcast.29, bf16[2,8,4,128,128]{4,3,2,1,0:T(8,128)(2,1)S(1)} %bitcast.24, ...), custom_call_target="tpu_custom_call" | custom-call | tf_op jit(solution)/shard_map/scatter/pallas_call | solution.py:453
  133.0 0.7 copy.16
  133.8 0.7 copy.17
  134.4 0.7 copy.18
  135.1 0.7 copy.19
  135.7 0.7 copy.20
  (8 shorter events, 0.0 us)
Async XLA Ops:
  1.5 75.8 %copy-start.13 = (s32[1,32]{1,0:T(1,128)S(1)}, s32[1,32]{1,0:T(1,128)}, u32[]{:S(2)}) copy-start(s32[1,32]{1,0:T(1,128)} %offsets.3) | copy-start | bytes 388
  50.3 2.2 %copy-start = (bf16[2,8,2,2,64,512]{5,4,3,2,1,0:T(8,128)(2,1)S(1)}, bf16[2,8,2,2,64,512]{5,4,3,2,1,0:T(8,128)(2,1)}, u32[]{:S(2)}) copy-start(bf16[2,8,2,2,64,512]{5,4,3,2,1,0:T(8,128)(2,1)} %get-tuple-element.25) | copy-start | bytes 12582916
  52.5 1.6 %copy-start.1 = (bf16[2,8,4,128,128]{4,3,2,1,0:T(8,128)(2,1)S(1)}, bf16[2,8,4,128,128]{4,3,2,1,0:T(8,128)(2,1)}, u32[]{:S(2)}) copy-start(bf16[2,8,4,128,128]{4,3,2,1,0:T(8,128)(2,1)} %get-tuple-element.24) | copy-start | bytes 6291460
  54.0 1.2 copy-start.3
  55.3 0.9 copy-start.5
  56.2 0.7 copy-start.12
  56.8 20.4 %copy-start.2 = (bf16[2,8,4,128,128]{4,3,2,1,0:T(8,128)(2,1)S(1)}, bf16[2,8,4,128,128]{4,3,2,1,0:T(8,128)(2,1)}, u32[]{:S(2)}) copy-start(bf16[2,8,4,128,128]{4,3,2,1,0:T(8,128)(2,1)} %get-tuple-element.24) | copy-start | bytes 6291460
  56.8 20.4 %copy-start.4 = (bf16[4,128,1024]{2,1,0:T(8,128)(2,1)S(1)}, bf16[4,128,1024]{2,1,0:T(8,128)(2,1)}, u32[]{:S(2)}) copy-start(bf16[4,128,1024]{2,1,0:T(8,128)(2,1)} %get-tuple-element.26.ogf) | copy-start | bytes 3145732
  56.8 20.4 %copy-start.6 = (bf16[4,128,128]{2,1,0:T(8,128)(2,1)S(1)}, bf16[4,128,128]{2,1,0:T(8,128)(2,1)}, u32[]{:S(2)}) copy-start(bf16[4,128,128]{2,1,0:T(8,128)(2,1)} %get-tuple-element.23) | copy-start | bytes 393220
  68.7 0.7 copy-start.7
  69.4 0.7 copy-start.11
  77.3 0.9 copy-start.8
  78.2 0.9 copy-start.9
  79.1 0.9 copy-start.10

commit v2 on v1

v2 whole, which is shorter than its diff:
```python
import jax
import jax.numpy as jnp
from jax import lax
from jax.experimental import pallas as pl
from jax.experimental.pallas import tpu as pltpu
from jax.sharding import PartitionSpec as P

HD = 128
MASKED = -1e30
MESH = pl.DeviceIdType.MESH
BF = jnp.bfloat16
F32 = jnp.float32
PHASES = ((-1, 1), (-2, 2), (-3, 3), (4,))


class Place:
    def __init__(self):
        self.dp = lax.axis_index("dp")
        self.ctx = lax.axis_index("ctx")
        self.mp = lax.axis_index("mp")
        self.z = self.ctx // 4
        self.j = self.ctx % 4
        self.yhi = self.j // 2
        self.core = self.j % 2
        self.y = self.yhi * 2 + self.dp

    def plane(self, off):
        return (self.z + 8 + off) % 8

    def yblock(self, off):
        y = (self.y + 4 + off) % 4
        return y % 2, y // 2

    def at_z(self, off):
        return {"ctx": self.plane(off) * 4 + self.j}

    def at_y(self, off):
        dp, yhi = self.yblock(off)
        return {"dp": dp, "ctx": self.z * 4 + yhi * 2 + self.core}

    def at_x(self, off):
        return {"mp": (self.mp + 4 + off) % 4}

    def at_j(self, off):
        return {"ctx": self.z * 4 + (self.j + 4 + off) % 4}

    def sibling(self):
        return {"ctx": self.ctx + 1 - 2 * self.core}


def greet(devices):
    barrier = pltpu.get_barrier_semaphore()
    for device in devices:
        pl.semaphore_signal(barrier, inc=1, device_id=device, device_id_type=MESH)
    pl.semaphore_wait(barrier, len(devices))


class Links:
    def __init__(self, send_sems, recv_sems):
        self.send_sems, self.recv_sems = send_sems, recv_sems
        self.slots = {}
        self.sent = []

    def slot(self, name):
        return self.slots.setdefault(name, len(self.slots))

    def copy(self, name, src, dst, device):
        i = self.slot(name)
        return pltpu.make_async_remote_copy(
            src_ref=src, dst_ref=dst, send_sem=self.send_sems.at[i],
            recv_sem=self.recv_sems.at[i], device_id=device, device_id_type=MESH)

    def send(self, name, src, dst, device):
        copy = self.copy(name, src, dst, device)
        copy.start()
        self.sent.append(copy)

    def wait(self, name, dst, device):
        self.copy(name, dst, dst, device).wait_recv()

    def drain(self):
        for copy in self.sent:
            copy.wait_send()


def any_spec(n):
    return [pl.BlockSpec(memory_space=pl.ANY)] * n


GROUPS = ((4,), (3, -3), (2, -2), (1, -1), (0,))
LOG2E = 1.4426950408889634
SCALE = HD ** -0.5
SCALE2 = SCALE * LOG2E
NT = (((1,), (1,)), ((), ()))
TN = (((0,), (0,)), ((), ()))
SIDES = ((0, 1), (1, -1))
SEMS = 176


def dot(a, b, dims=(((1,), (0,)), ((), ()))):
    return lax.dot_general(a, b, dims, preferred_element_type=F32)


def plus(*terms):
    total = terms[0].astype(F32)
    for term in terms[1:]:
        total = total + term.astype(F32)
    return total


def kernel(offsets, q, k, v, w, og, proj, dq, dk, dv, wg,
           qh, kv, wf, ogf, doh, atth, ghs, att_tok, dqh, dkv, px, wgp,
           zr, zs, zfin, xr0, xs, xr1, projs, sibr, wsum, yr0, yr1, wy, wzr, wzs, wgs,
           acc, top, norm, sc, pb, gacc, lse, delta, posq, qacc,
           send_sems, recv_sems, local_sems):
    at = Place()
    z, j, core, mp = at.z, at.j, at.core, at.mp
    greet([at.at_j(1), at.at_j(2), at.at_j(3), at.at_z(1), at.at_z(-1),
           at.at_y(1), at.at_y(-1), at.at_x(1), at.at_x(-1)])
    links = Links(send_sems, recv_sems)

    def head(ref, off):
        return ref.at[:, pl.ds(pl.multiple_of((j + 4 + off) % 4 * HD, HD), HD)]

    def wblock(zoff, yoff, half=None):
        dp, yhi = at.yblock(yoff)
        ref = wf.at[dp, at.plane(zoff), yhi, core]
        return ref if half is None else ref.at[pl.ds(half * 32, 32)]

    own = [
        pltpu.make_async_copy(head(k, 0), kv.at[0, z, j], local_sems.at[0]),
        pltpu.make_async_copy(head(v, 0), kv.at[1, z, j], local_sems.at[1]),
        pltpu.make_async_copy(w, wblock(0, 0), local_sems.at[2]),
        pltpu.make_async_copy(head(q, 0), qh.at[j], local_sems.at[3]),
        pltpu.make_async_copy(og, ogf.at[mp], local_sems.at[4]),
    ]

    def wstep(s):
        for i, d in SIDES:
            off = -d * (1 + s)
            if s < 3:
                links.wait(("wz", d, s), wblock(off, 0), at.at_z(d))
            else:
                links.wait(("wz", d, s), wblock(4, 0, i), at.at_z(d))
            if s < 2:
                links.send(("wz", d, s + 1), wblock(off, 0), wblock(off, 0), at.at_z(d))
            elif s == 2:
                links.send(("wz", d, 3), wblock(off, 0, i), wblock(off, 0, i), at.at_z(d))
        for off in PHASES[s]:
            for d in (1, -1):
                links.send(("wy", off, d), wblock(off, 0), wblock(off, 0), at.at_y(d))

    def forward_y(*offs):
        for off in offs:
            for i, d in SIDES:
                links.wait(("wy", off, d), wblock(off, -d), at.at_y(d))
                links.send(("wyh", off, d), wblock(off, -d, i), wblock(off, -d, i), at.at_y(d))

    def to_sibling(*offs):
        for off in offs:
            for i, d in SIDES:
                links.wait(("wyh", off, d), wblock(off, 2, i), at.at_y(d))
            for dp in (0, 1):
                ref = wf.at[dp, at.plane(off), :, core]
                links.send(("sib", off, dp), ref, ref, at.sibling())

    def ring(a, s):
        for i, d in SIDES:
            if s == 3 and a != i:
                continue
            chunk = kv.at[a, at.plane(-d * (1 + s))]
            links.wait(("z", a, d, s), chunk, at.at_z(d))
            if s < 2 or (s == 2 and a == i):
                links.send(("z", a, d, s + 1), chunk, chunk, at.at_z(d))

    row_in = lax.broadcasted_iota(jnp.int32, (128, 512), 0)

    def allowed(plane, i):
        return row_in <= posq[...] - offsets[0, plane * 4 + i] * 128

    def scores(*offs):
        qs = qh[...].reshape(512, HD)
        best = top[...]
        for n, off in enumerate(offs):
            plane = at.plane(off)

            def tile(i, best):
                s = dot(kv[0, plane, i], qs, NT) * SCALE2
                s = jnp.where(allowed(plane, i), s, MASKED)
                sc[n, i] = s
                return jnp.maximum(best, jnp.max(s.reshape(16, 8, 512), axis=0))

            best = lax.fori_loop(0, 4, tile, best)
        m = jnp.max(best, axis=0, keepdims=True)
        alpha = jnp.exp2(top[0:1] - m)
        top[...] = jnp.broadcast_to(m, (8, 512))
        total = norm[...] * alpha
        for n, off in enumerate(offs):

            def lift(i, total):
                p = jnp.exp2(sc[n, i] - m)
                pb[n, i] = p.astype(BF)
                return total + jnp.sum(p.reshape(16, 8, 512), axis=0)

            total = lax.fori_loop(0, 4, lift, total)
        norm[...] = total
        acc[...] = acc[...] * alpha

    def weigh(*offs):
        for n, off in enumerate(offs):
            values = kv[1, at.plane(off)].reshape(512, HD)
            acc[...] += dot(values, pb[n].reshape(512, 512), TN)

    def og_cols(dp, plane):
        cols = pl.ds(pl.multiple_of(plane % 4 * 256, 256), 256)
        return ogf[dp * 2 + plane // 4, :, cols]

    def head_grad(*offs):
        for off in offs:
            plane = at.plane(off)
            for dp in (0, 1):
                ref = wf.at[dp, plane, :, 1 - core]
                links.wait(("sib", off, dp), ref, at.sibling())
                gacc[...] += dot(og_cols(dp, plane), wf[dp, plane].reshape(256, 512))

    for copy in own:
        copy.start()
    for a, ref in ((0, k), (1, v)):
        for t in (1, 2, 3):
            links.send(("kv", a, t), head(ref, t), kv.at[a, z, j], at.at_j(t))
    for d in (1, -1):
        links.send(("wz", d, 0), w, wblock(0, 0), at.at_z(d))
        links.send(("wy", 0, d), w, wblock(0, 0), at.at_y(d))
    for t in (1, 2, 3):
        links.send(("q", t), head(q, t), qh.at[j], at.at_j(t))
    for d in (1, -1):
        links.send(("og", d, 0), og, ogf.at[mp], at.at_x(d))
    lane = lax.broadcasted_iota(jnp.int32, (1, 512), 1)
    place = lane % 128
    for i in range(4):
        place = place + jnp.where(lane // 128 == i, offsets[0, z * 4 + i] * 128, 0)
    posq[...] = place
    acc[...] = jnp.zeros_like(acc)
    gacc[...] = jnp.zeros_like(gacc)
    qacc[...] = jnp.zeros_like(qacc)
    norm[...] = jnp.zeros_like(norm)
    top[...] = jnp.full_like(top, MASKED)

    for a in (0, 1):
        own[a].wait()
        for t in (1, 2, 3):
            links.wait(("kv", a, t), kv.at[a, z, (j + 4 - t) % 4], at.at_j(t))
        for d in (1, -1):
            links.send(("z", a, d, 0), kv.at[a, z], kv.at[a, z], at.at_z(d))
    own[2].wait()
    wstep(0)
    own[3].wait()
    for t in (1, 2, 3):
        links.wait(("q", t), qh.at[(j + 4 - t) % 4], at.at_j(t))
    scores(0)
    weigh(0)
    wstep(1)
    forward_y(0)
    ring(0, 0)
    scores(-1, 1)
    own[4].wait()
    for i, d in SIDES:
        links.wait(("og", d, 0), ogf.at[(mp + 4 - d) % 4], at.at_x(d))
        half = ogf.at[(mp + 4 - d) % 4, pl.ds(i * 64, 64)]
        links.send(("og", d, 1), half, half, at.at_x(d))
    ring(1, 0)
    wstep(2)
    forward_y(-1, 1)
    weigh(-1, 1)
    to_sibling(0)
    ring(0, 1)
    scores(-2, 2)
    wstep(3)
    ring(1, 1)
    forward_y(-2, 2)
    weigh(-2, 2)
    to_sibling(-1, 1)
    for i, d in SIDES:
        half = ogf.at[(mp + 2) % 4, pl.ds(i * 64, 64)]
        links.wait(("og", d, 1), half, at.at_x(d))
    head_grad(0)
    ring(0, 2)
    scores(-3, 3)
    forward_y(-3, 3)
    to_sibling(-2, 2)
    ring(1, 2)
    weigh(-3, 3)
    forward_y(4)
    to_sibling(-3, 3)
    head_grad(-1, 1, -2, 2)
    to_sibling(4)
    ring(0, 3)
    scores(4)
    head_grad(-3, 3, 4)
    ghs[...] = gacc[...].astype(BF)
    for t in (1, 2, 3):
        links.send(("g", t), head(ghs, t), doh.at[j], at.at_j(t))
    own.append(pltpu.make_async_copy(head(ghs, 0), doh.at[j], local_sems.at[5]))
    own[5].start()
    ring(1, 3)
    weigh(4)
    total = jnp.sum(norm[...], axis=0, keepdims=True)
    atth[...] = (acc[...] / total).T.astype(BF).reshape(4, 128, HD)
    lse[...] = top[0:1] + jnp.log2(total)
    for t in (1, 2, 3):
        links.send(("a", t), atth.at[(j + t) % 4], head(att_tok, 0), at.at_j(t))
    own.append(pltpu.make_async_copy(atth.at[j], head(att_tok, 0), local_sems.at[6]))
    own[6].start()

    def backward(off):
        plane = at.plane(off)
        qs = qh[...].reshape(512, HD)
        do = doh[...].reshape(512, HD)

        def tile(i, carry):
            kt, vt = kv[0, plane, i], kv[1, plane, i]
            s = dot(kt, qs, NT) * SCALE2
            p = jnp.where(allowed(plane, i), jnp.exp2(s - lse[...]), 0.0)
            ds = (p * (dot(vt, do, NT) - delta[...])).astype(BF)
            dkv[1, plane, i] = dot(p.astype(BF), do).astype(BF)
            dkv[0, plane, i] = (dot(ds, qs) * SCALE).astype(BF)
            qacc[...] += dot(kt, ds, TN)
            return carry

        lax.fori_loop(0, 4, tile, 0)

    def zsend(s, raw=None):
        for i, d in SIDES:
            for a in (0, 1):
                if s == 0 and a != i:
                    continue
                if raw is not None and raw != (a != i):
                    continue
                p = at.plane(d * (4 - s))
                if s == 0 or (s == 1 and a != i):
                    src = dkv.at[a, p]
                else:
                    links.wait(("rz", a, d, s - 1), zr.at[a, i, s - 1], at.at_z(d))
                    zs[a, i, s - 1] = plus(dkv[a, p], zr[a, i, s - 1]).astype(BF)
                    src = zs.at[a, i, s - 1]
                links.send(("rz", a, d, s), src, zr.at[a, i, s], at.at_z(d))

    def zfinal():
        for a, out in ((0, dk), (1, dv)):
            for i, d in SIDES:
                links.wait(("rz", a, d, 3), zr.at[a, i, 3], at.at_z(d))
            zfin[a] = plus(dkv[a, z], zr[a, 0, 3], zr[a, 1, 3]).astype(BF)
            for t in (1, 2, 3):
                links.send(("dkv", a, t), zfin.at[a, (j + t) % 4], head(out, 0), at.at_j(t))
            copy = pltpu.make_async_copy(zfin.at[a, j], head(out, 0), local_sems.at[7 + a])
            copy.start()
            own.append(copy)

    def project(off):
        x = (mp + 4 + off) % 4
        rows = wf[x // 2, pl.ds(pl.multiple_of(x % 2 * 4, 4), 4)].reshape(1024, 512)
        px[x] = dot(att_tok[...], rows, NT).astype(BF)

    def xfirst():
        for i, d in SIDES:
            links.send(("x", d, 0), px.at[(mp + 2) % 4, pl.ds(i * 64, 64)], xr0.at[i], at.at_x(d))

    def xsecond():
        for i, d in SIDES:
            chunk = (mp + 4 + d) % 4
            links.wait(("x", d, 0), xr0.at[i], at.at_x(d))
            xs[i, pl.ds(i * 64, 64)] = plus(px[chunk, pl.ds(i * 64, 64)], xr0[i]).astype(BF)
            xs[i, pl.ds(64 - i * 64, 64)] = px[chunk, pl.ds(64 - i * 64, 64)]
            links.send(("x", d, 1), xs.at[i], xr1.at[i], at.at_x(d))

    def xfinal():
        for i, d in SIDES:
            links.wait(("x", d, 1), xr1.at[i], at.at_x(d))
        projs[...] = plus(px[mp], xr1[0], xr1[1]).astype(BF)
        copy = pltpu.make_async_copy(projs, proj, local_sems.at[9])
        copy.start()
        own.append(copy)

    def weight_grad(*offs):
        for off in offs:
            p = at.plane(off)
            for dp in (0, 1):
                part = dot(og_cols(dp, p), att_tok[...], TN).astype(BF)
                wgp[dp, p] = part.reshape(2, 2, 64, 512)
                links.send(("wsib", off, dp), wgp.at[dp, p, :, 1 - core], sibr.at[dp, p], at.sibling())

    def yfirst(off):
        p = at.plane(off)
        for dp in (0, 1):
            links.wait(("wsib", off, dp), sibr.at[dp, p], at.sibling())
        for dp in (0, 1):
            for yhi in (0, 1):
                wsum[dp, p, yhi] = plus(wgp[dp, p, yhi, core], sibr[dp, p, yhi]).astype(BF)
        dp, yhi = at.yblock(2)
        for i, d in SIDES:
            links.send(("y", off, d, 0), wsum.at[dp, p, yhi, pl.ds(i * 32, 32)], yr0.at[p, i], at.at_y(d))

    def ysecond(off):
        p = at.plane(off)
        for i, d in SIDES:
            dp, yhi = at.yblock(d)
            links.wait(("y", off, d, 0), yr0.at[p, i], at.at_y(d))
            rows = pl.ds(i * 32, 32)
            wsum[dp, p, yhi, rows] = plus(wsum[dp, p, yhi, rows], yr0[p, i]).astype(BF)
            links.send(("y", off, d, 1), wsum.at[dp, p, yhi], yr1.at[p, i], at.at_y(d))

    def yfinal(off):
        p = at.plane(off)
        for i, d in SIDES:
            links.wait(("y", off, d, 1), yr1.at[p, i], at.at_y(d))
        total = plus(wsum[at.dp, p, at.yhi], yr1[p, 0], yr1[p, 1])
        if off == 0:
            for i, d in SIDES:
                links.wait(("w", d, 3), wzr.at[i, 3], at.at_z(d))
            wgs[...] = plus(total, wzr[0, 3], wzr[1, 3])
            copy = pltpu.make_async_copy(wgs, wg, local_sems.at[10])
            copy.start()
            own.append(copy)
            return
        if off == 4:
            wy[...] = total.astype(BF)
            for i, d in SIDES:
                rows = pl.ds(i * 32, 32)
                links.send(("w", d, 0), wy.at[rows], wzr.at[i, 0, rows], at.at_z(d))
            return
        d = 1 if off > 0 else -1
        i = (1 - d) // 2
        s = 4 - abs(off)
        if s == 1:
            rows = pl.ds(i * 32, 32)
            links.wait(("w", d, 0), wzr.at[i, 0, rows], at.at_z(d))
            wzs[i, 0] = total.astype(BF)
            wzs[i, 0, rows] = plus(total[i * 32:i * 32 + 32], wzr[i, 0, rows]).astype(BF)
        else:
            links.wait(("w", d, s - 1), wzr.at[i, s - 1], at.at_z(d))
            wzs[i, s - 1] = plus(total, wzr[i, s - 1]).astype(BF)
        links.send(("w", d, s), wzs.at[i, s - 1], wzr.at[i, s], at.at_z(d))

    def each(step, group):
        for off in GROUPS[group]:
            step(off)

    own[5].wait()
    for t in (1, 2, 3):
        links.wait(("g", t), doh.at[(j + 4 - t) % 4], at.at_j(t))
    products = (doh[...].astype(F32) * atth[...].astype(F32)).reshape(512, HD)
    delta[...] = jnp.sum(products.T, axis=0, keepdims=True)
    backward(4)
    zsend(0)
    own[6].wait()
    for t in (1, 2, 3):
        links.wait(("a", t), head(att_tok, -t), at.at_j(t))
    weight_grad(4, 3, -3)
    project(2)
    xfirst()
    backward(3)
    backward(-3)
    zsend(1, True)
    weight_grad(2, -2, 1, -1, 0)
    each(yfirst, 0)
    project(1)
    project(-1)
    zsend(1, False)
    each(yfirst, 1)
    xsecond()
    backward(2)
    each(ysecond, 0)
    backward(-2)
    each(yfirst, 2)
    each(ysecond, 1)
    zsend(2)
    each(yfinal, 0)
    backward(1)
    each(yfirst, 3)
    backward(-1)
    each(ysecond, 2)
    each(yfinal, 1)
    zsend(3)
    project(0)
    xfinal()
    each(yfirst, 4)
    backward(0)
    each(ysecond, 3)
    each(yfinal, 2)
    dqh[...] = (qacc[...] * SCALE).T.astype(BF).reshape(4, 128, HD)
    for t in (1, 2, 3):
        links.send(("dq", t), dqh.at[(j + t) % 4], head(dq, 0), at.at_j(t))
    copy = pltpu.make_async_copy(dqh.at[j], head(dq, 0), local_sems.at[11])
    copy.start()
    own.append(copy)
    each(ysecond, 4)
    zfinal()
    each(yfinal, 3)
    each(yfinal, 4)
    for t in (1, 2, 3):
        links.wait(("dq", t), head(dq, -t), at.at_j(t))
        links.wait(("dkv", 0, t), head(dk, -t), at.at_j(t))
        links.wait(("dkv", 1, t), head(dv, -t), at.at_j(t))
    for copy in own[7:]:
        copy.wait()
    links.drain()
    assert len(links.slots) <= SEMS, len(links.slots)


def on_device(queries, key_rows, value_rows, out_weight, out_grad, block_offsets):
    heads = jax.ShapeDtypeStruct((128, 512), BF)
    proj, dq, dk, dv, wg = pl.pallas_call(
        kernel,
        out_shape=(
            jax.ShapeDtypeStruct((128, 1024), BF), heads, heads, heads,
            jax.ShapeDtypeStruct((64, 512), F32),
        ),
        in_specs=[pl.BlockSpec(memory_space=pltpu.SMEM)] + any_spec(5),
        out_specs=tuple(any_spec(5)),
        scratch_shapes=[
            pltpu.VMEM((4, 128, HD), BF),
            pltpu.VMEM((2, 8, 4, 128, HD), BF),
            pltpu.VMEM((2, 8, 2, 2, 64, 512), BF),
            pltpu.VMEM((4, 128, 1024), BF),
            pltpu.VMEM((4, 128, HD), BF),
            pltpu.VMEM((4, 128, HD), BF),
            pltpu.VMEM((128, 512), BF),
            pltpu.VMEM((128, 512), BF),
            pltpu.VMEM((4, 128, HD), BF),
            pltpu.VMEM((2, 8, 4, 128, HD), BF),
            pltpu.VMEM((4, 128, 1024), BF),
            pltpu.VMEM((2, 8, 2, 2, 64, 512), BF),
            pltpu.VMEM((2, 2, 4, 4, 128, HD), BF),
            pltpu.VMEM((2, 2, 3, 4, 128, HD), BF),
            pltpu.VMEM((2, 4, 128, HD), BF),
            pltpu.VMEM((2, 64, 1024), BF),
            pltpu.VMEM((2, 128, 1024), BF),
            pltpu.VMEM((2, 128, 1024), BF),
            pltpu.VMEM((128, 1024), BF),
            pltpu.VMEM((2, 8, 2, 64, 512), BF),
            pltpu.VMEM((2, 8, 2, 64, 512), BF),
            pltpu.VMEM((8, 2, 32, 512), BF),
            pltpu.VMEM((8, 2, 64, 512), BF),
            pltpu.VMEM((64, 512), BF),
            pltpu.VMEM((2, 4, 64, 512), BF),
            pltpu.VMEM((2, 3, 64, 512), BF),
            pltpu.VMEM((64, 512), F32),
            pltpu.VMEM((HD, 512), F32),
            pltpu.VMEM((8, 512), F32),
            pltpu.VMEM((8, 512), F32),
            pltpu.VMEM((2, 4, 128, 512), F32),
            pltpu.VMEM((2, 4, 128, 512), BF),
            pltpu.VMEM((128, 512), F32),
            pltpu.VMEM((1, 512), F32),
            pltpu.VMEM((1, 512), F32),
            pltpu.VMEM((1, 512), jnp.int32),
            pltpu.VMEM((HD, 512), F32),
            pltpu.SemaphoreType.DMA((SEMS,)),
            pltpu.SemaphoreType.DMA((SEMS,)),
            pltpu.SemaphoreType.DMA((12,)),
        ],
        compiler_params=pltpu.CompilerParams(
            collective_id=0, has_side_effects=True, vmem_limit_bytes=62 << 20),
        name="whole",
    )(block_offsets, queries[0], key_rows[0], value_rows[0], out_weight, out_grad[0])
    return proj[None], dq[None], dk[None], dv[None], wg


def solution(mesh):
    tokens = P("dp", "ctx", "mp")
    features = P(("dp", "ctx"), "mp")
    return jax.shard_map(
        on_device,
        mesh=mesh,
        in_specs=(tokens, tokens, tokens, features, tokens, P("dp", None)),
        out_specs=(tokens, tokens, tokens, tokens, features),
        check_vma=False,
    )
```

time: 137 us -> 97.2 us (0.71)
  Pallas kernels: 121 us -> 91.1 us
  local copies, waits for them, and re-layouts: 13.9 us -> 5.21 us
    pallas_call x5 -> x1, Pallas kernels: 121 us -> 91.1 us  [on_device(): pl.pallas_call(kernel, out_shape=(jax.ShapeDtypeStruct((128, 1024), BF),...]
    unnamed x33 -> x13, local copies, waits for them, and re-layouts: 13.9 us -> 5.21 us
where the time goes in v2:
time: 97.2 us; the launch traced here: 97 us
  Pallas kernels  91.1 us (94%)
  local copies, waits for them, and re-layouts  5.21 us (5%)
    pallas_call x1, Pallas kernels, on_device(): pl.pallas_call(kernel, out_shape=(jax.ShapeDtypeStruct((128, 1024), BF),...  91.1 us
    unnamed x13, local copies, waits for them, and re-layouts  5.21 us

profile of v2, /device:TPU:1, one launch (start us, length us, event | category | flops | bytes accessed | tf_op | source)
XLA Modules:
  0.0 97.0 jit_solution(1899727067145157304)
XLA Ops:
  0.6 91.1 %whole.1 = (bf16[128,1024]{1,0:T(8,128)(2,1)}, bf16[128,512]{1,0:T(8,128)(2,1)}, bf16[128,512]{1,0:T(8,128)(2,1)}, bf16[128,512]{1,0:T(8,128)(2,1)}, f32[64,512]{1,0:T(8,128)}) custom-call(s32[1,32]{1,0:T(1,128)} %offsets.1, bf16[128,512]{1,0:T(8,128)(2,1)} %bitcast.10, bf16[128,512]{1,0:T(8,128)(2,1)} %bitcast.11, bf16[128,512]{1,0:T(8,128)(2,1)} %bitcast.12, ...), custom_call_target="tpu_custom_call" | custom-call | tf_op jit(solution)/shard_map/whole/pallas_call | solution.py:512
  91.8 0.0 copy-start.3
  91.8 1.7 %copy.16 = bf16[1,128,1024]{2,1,0:T(8,128)(2,1)} copy(bf16[1,128,1024]{2,1,0:T(8,128)(2,1)} %bitcast.9) | data formatting | bytes 524288
  93.5 0.0 copy-done.3
  93.5 0.0 copy-start.2
  93.5 0.7 copy.17
  94.2 0.3 copy-done.2
  94.5 0.0 copy-start.1
  94.5 0.7 copy.18
  95.1 0.3 copy-done.1
  95.4 0.0 copy-start
  95.4 0.7 copy.19
  96.1 0.3 copy-done
  96.4 0.7 copy.20
Async XLA Ops:
  91.8 1.7 %copy-start.3 = (bf16[128,512]{1,0:T(8,128)(2,1)S(1)}, bf16[128,512]{1,0:T(8,128)(2,1)}, u32[]{:S(2)}) copy-start(bf16[128,512]{1,0:T(8,128)(2,1)} %get-tuple-element.11) | copy-start | bytes 393220
  93.5 1.0 copy-start.2
  94.5 1.0 copy-start.1
  95.4 1.0 copy-start

commit v3 on v2

v3 whole, which is shorter than its diff:
```python
import jax
import jax.numpy as jnp
from jax import lax
from jax.experimental import pallas as pl
from jax.experimental.pallas import tpu as pltpu
from jax.sharding import PartitionSpec as P

HD = 128
MASKED = -1e30
MESH = pl.DeviceIdType.MESH
BF = jnp.bfloat16
F32 = jnp.float32
PHASES = ((-1, 1), (-2, 2), (-3, 3), (4,))


class Place:
    def __init__(self):
        self.dp = lax.axis_index("dp")
        self.ctx = lax.axis_index("ctx")
        self.mp = lax.axis_index("mp")
        self.z = self.ctx // 4
        self.j = self.ctx % 4
        self.yhi = self.j // 2
        self.core = self.j % 2
        self.y = self.yhi * 2 + self.dp

    def plane(self, off):
        return (self.z + 8 + off) % 8

    def yblock(self, off):
        y = (self.y + 4 + off) % 4
        return y % 2, y // 2

    def at_z(self, off):
        return {"ctx": self.plane(off) * 4 + self.j}

    def at_y(self, off):
        dp, yhi = self.yblock(off)
        return {"dp": dp, "ctx": self.z * 4 + yhi * 2 + self.core}

    def at_x(self, off):
        return {"mp": (self.mp + 4 + off) % 4}

    def at_j(self, off):
        return {"ctx": self.z * 4 + (self.j + 4 + off) % 4}

    def sibling(self):
        return {"ctx": self.ctx + 1 - 2 * self.core}


def greet(devices):
    barrier = pltpu.get_barrier_semaphore()
    for device in devices:
        pl.semaphore_signal(barrier, inc=1, device_id=device, device_id_type=MESH)
    pl.semaphore_wait(barrier, len(devices))


class Links:
    def __init__(self, send_sems, recv_sems):
        self.send_sems, self.recv_sems = send_sems, recv_sems
        self.slots = {}
        self.leaving = [None] * SENDS
        self.count = 0

    def copy(self, name, src, dst, device, sender):
        i = self.slots.setdefault(name, len(self.slots))
        return pltpu.make_async_remote_copy(
            src_ref=src, dst_ref=dst, send_sem=self.send_sems.at[sender],
            recv_sem=self.recv_sems.at[i], device_id=device, device_id_type=MESH)

    def send(self, name, src, dst, device):
        i = self.count % SENDS
        self.count += 1
        if self.leaving[i] is not None:
            self.leaving[i].wait_send()
        self.leaving[i] = self.copy(name, src, dst, device, i)
        self.leaving[i].start()

    def wait(self, name, dst, device):
        self.copy(name, dst, dst, device, 0).wait_recv()

    def drain(self):
        for copy in self.leaving:
            copy.wait_send()


def vmem(n):
    return [pl.BlockSpec(memory_space=pltpu.VMEM)] * n


def any_spec(n):
    return [pl.BlockSpec(memory_space=pl.ANY)] * n


GROUPS = ((4,), (3, -3), (2, -2), (1, -1), (0,))
LOG2E = 1.4426950408889634
SCALE = HD ** -0.5
SCALE2 = SCALE * LOG2E
NT = (((1,), (1,)), ((), ()))
TN = (((0,), (0,)), ((), ()))
SIDES = ((0, 1), (1, -1))
SENDS = 32
RECEIVES = 131
ORDER = (
    ("K0",), ("W0",), ("WY0",), ("Q0",), ("W", 0, -1),
    ("W", 0, 1), ("OG0",), ("V0",), ("WY", 1), ("WY", -1),
    ("RA", 0), ("W", 1, 1), ("FY", 0, 1), ("FY", 0, -1), ("W", 1, -1),
    ("WY", 2), ("WY", -2), ("RA", 1), ("W", 2, -1), ("W", 2, 1),
    ("R", 0, 0, -1), ("WY", -3), ("SC", 0), ("R", 0, 0, 1), ("FY", 1, -1),
    ("FY", -2, 1), ("WY", 3), ("OG", 1), ("R", 1, 0, 1), ("W", 3, -1),
    ("FY", 2, 1), ("FY", -1, -1), ("FY", -1, 1), ("R", 1, 0, -1), ("W", 3, 1),
    ("OG", -1), ("WE", 0), ("FY", -2, -1), ("FY", 1, 1), ("SC", 1),
    ("FY", -3, -1), ("R", 0, 1, -1), ("WY", 4), ("S", 0), ("R", 0, 1, 1),
    ("FY", 2, -1), ("FY", -3, 1), ("WE", 1), ("S", -1), ("FY", 3, -1),
    ("FY", 3, 1), ("R", 1, 1, 1), ("FY", 4, -1), ("S", -2), ("R", 1, 1, -1),
    ("FY", 4, 1), ("S", 2), ("SC", 2), ("OL",), ("HG", -2),
    ("S", -3), ("S", 3), ("S", 1), ("HG", 2), ("R", 0, 2, 1),
    ("HG", 0), ("S", 4), ("HG", -1), ("R", 0, 2, -1), ("HG", -3),
    ("R", 1, 2, -1), ("WE", 2), ("HG", 1), ("HG", 4), ("HG", 3),
    ("GH",), ("R", 1, 2, 1), ("SC", 3), ("R", 0, 3, 1), ("WE", 3),
    ("SC", 4), ("R", 1, 3, -1), ("WE", 4), ("FIN",), ("DEL",),
    ("B", 4), ("Z", 1, 0, -1), ("Z", 0, 0, 1), ("B", 3), ("B", -3),
    ("Z", 0, 1, -1), ("Z", 1, 1, 1), ("B", 2), ("ATT",), ("WG", 4),
    ("WG", 3), ("WG", -3), ("WG", 2), ("B", -2), ("Y1", 4),
    ("Z", 1, 1, -1), ("Z", 0, 1, 1), ("WG", -2), ("Y1", -3), ("Y1", 3),
    ("WG", -1), ("Y1", 2), ("WG", 1), ("Z", 0, 2, -1), ("Y1", -2),
    ("Z", 1, 2, 1), ("Y2", 4, 1), ("WG", 0), ("Y2", 4, -1), ("PX", 2),
    ("Y2", -3, 1), ("Y1", -1), ("Y2", -3, -1), ("Y1", 1), ("Z", 1, 2, -1),
    ("Z", 0, 2, 1), ("Y2", 3, -1), ("PX", 1), ("B", -1), ("XF",),
    ("Y2", 3, 1), ("B", 1), ("Y3", 4), ("Z", 0, 3, -1), ("Y2", -2, 1),
    ("Z", 1, 3, 1), ("Y2", 2, 1), ("Y1", 0), ("Y2", -2, -1), ("B", 0),
    ("Y2", 1, 1), ("Y2", 2, -1), ("DQ",), ("Y2", -1, 1), ("Y3", -3),
    ("Y3", 3), ("PX", -1), ("Y2", 1, -1), ("Z", 1, 3, -1), ("XS", -1),
    ("Z", 0, 3, 1), ("XS", 1), ("Y2", -1, -1), ("Y2", 0, -1), ("Y2", 0, 1),
    ("Y3", 2), ("Y3", -2), ("ZF", 1), ("PX", 0), ("ZF", 0),
    ("Y3", -1), ("Y3", 1), ("XE",), ("Y3", 0), ("END",),
)


def dot(a, b, dims=(((1,), (0,)), ((), ()))):
    return lax.dot_general(a, b, dims, preferred_element_type=F32)


def plus(*terms):
    total = terms[0].astype(F32)
    for term in terms[1:]:
        total = total + term.astype(F32)
    return total


def kernel(offsets, q, k, v, w, og, proj, dq, dk, dv, wg,
           qh, kv, wf, ogf, doh, atth, ghs, att_tok, dqh, dkv, px, wgp,
           zr, zs, zfin, xr0, xs, xr1, projs, sibr, wsum, yr0, yr1, wyb, wzr, wzs, wgs,
           acc, top, norm, sc, pb, gacc, lse, delta, posq, qacc,
           send_sems, recv_sems, local_sems):
    at = Place()
    z, j, core, mp = at.z, at.j, at.core, at.mp
    greet([at.at_j(1), at.at_j(2), at.at_j(3), at.at_z(1), at.at_z(-1),
           at.at_y(1), at.at_y(-1), at.at_x(1), at.at_x(-1)])
    links = Links(send_sems, recv_sems)

    def head(ref, off):
        return ref.at[:, pl.ds(pl.multiple_of((j + 4 + off) % 4 * HD, HD), HD)]

    def wblock(zoff, yoff, half=None):
        dp, yhi = at.yblock(yoff)
        ref = wf.at[dp, at.plane(zoff), yhi, core]
        return ref if half is None else ref.at[pl.ds(half * 32, 32)]

    own = {}

    def keep(name, src, dst):
        own[name] = pltpu.make_async_copy(src, dst, local_sems.at[len(own)])
        own[name].start()

    def scatter_heads(name, blocks, dst):
        for t in (1, 2, 3):
            links.send(name, blocks(t), dst, at.at_j(t))
        keep(name, blocks(0), dst)

    def await_heads(name, three):
        links.wait(name, three, at.at_j(1))
        own[name].wait()

    three_blocks = pl.ds(0, 3)
    three_heads = pl.ds(0, 3 * HD)

    def k0():
        scatter_heads("k", lambda t: head(k, t), kv.at[0, z, j])

    def v0():
        scatter_heads("v", lambda t: head(v, t), kv.at[1, z, j])

    def q0():
        scatter_heads("q", lambda t: head(q, t), qh.at[j])

    def w0():
        keep("w", w, wblock(0, 0))
        for d in (1, -1):
            links.send(("wz", d, 0), w, wblock(0, 0), at.at_z(d))

    def wy0():
        for d in (1, -1):
            links.send(("wy", 0, d), w, wblock(0, 0), at.at_y(d))

    def og0():
        for d in (1, -1):
            links.send(("og", d, 0), og, ogf.at[mp], at.at_x(d))
        keep("og", og, ogf.at[mp])

    def ring_start(a):
        await_heads("kv"[a], kv.at[a, z, three_blocks])
        for d in (1, -1):
            links.send(("z", a, d, 0), kv.at[a, z], kv.at[a, z], at.at_z(d))

    def ring(a, s, d):
        i = (1 - d) // 2
        chunk = kv.at[a, at.plane(-d * (1 + s))]
        links.wait(("z", a, d, s), chunk, at.at_z(d))
        if s < 2 or (s == 2 and a == i):
            links.send(("z", a, d, s + 1), chunk, chunk, at.at_z(d))

    def wstep(s, d):
        i = (1 - d) // 2
        block = wblock(-d * (1 + s), 0) if s < 3 else wblock(4, 0, i)
        links.wait(("wz", d, s), block, at.at_z(d))
        if s < 2:
            links.send(("wz", d, s + 1), block, block, at.at_z(d))
        elif s == 2:
            half = wblock(-d * 3, 0, i)
            links.send(("wz", d, 3), half, half, at.at_z(d))

    def wy(off):
        for d in (1, -1):
            links.send(("wy", off, d), wblock(off, 0), wblock(off, 0), at.at_y(d))

    def wforward(off, d):
        i = (1 - d) // 2
        links.wait(("wy", off, d), wblock(off, -d), at.at_y(d))
        links.send(("wyh", off), wblock(off, -d, i), wblock(off, -d, i), at.at_y(d))

    def wshare(off):
        if off == 0:
            own["w"].wait()
        links.wait(("wyh", off), wblock(off, 2), at.at_y(1))
        for dp in (0, 1):
            ref = wf.at[dp, at.plane(off), :, core]
            links.send(("sib", off), ref, ref, at.sibling())

    def ogstep(d):
        slot = ogf.at[(mp + 4 - d) % 4]
        links.wait(("og", d, 0), slot, at.at_x(d))
        half = slot.at[pl.ds((1 - d) // 2 * 64, 64)]
        links.send("ogh", half, half, at.at_x(d))

    def oglast():
        own["og"].wait()
        links.wait("ogh", ogf.at[(mp + 2) % 4], at.at_x(1))

    row_in = lax.broadcasted_iota(jnp.int32, (128, 512), 0)

    def allowed(plane):
        return jnp.concatenate(
            [row_in <= posq[...] - offsets[0, plane * 4 + i] * 128 for i in range(4)], axis=0)

    def fold(op, rows):
        return op(rows.reshape(64, 8, 512), axis=0)

    def begin():
        lane = lax.broadcasted_iota(jnp.int32, (1, 512), 1)
        place = lane % 128
        for i in range(4):
            place = place + jnp.where(lane // 128 == i, offsets[0, z * 4 + i] * 128, 0)
        posq[...] = place
        acc[...] = jnp.zeros_like(acc)
        gacc[...] = jnp.zeros_like(gacc)
        qacc[...] = jnp.zeros_like(qacc)
        norm[...] = jnp.zeros_like(norm)
        top[...] = jnp.full_like(top, MASKED)

    def planes(n):
        return (n,) if n in (0, 4) else (-n, n)

    def scores(n):
        if n == 0:
            begin()
            await_heads("q", qh.at[three_blocks])
        qs = qh[...].reshape(512, HD)
        best = top[...]
        for i, off in enumerate(planes(n)):
            plane = at.plane(off)
            s = dot(kv[0, plane].reshape(512, HD), qs, NT) * SCALE2
            s = jnp.where(allowed(plane), s, MASKED)
            sc[i] = s
            best = jnp.maximum(best, fold(jnp.max, s))
        m = jnp.max(best, axis=0, keepdims=True)
        alpha = jnp.exp2(top[0:1] - m)
        top[...] = jnp.broadcast_to(m, (8, 512))
        total = norm[...] * alpha
        for i, off in enumerate(planes(n)):
            p = jnp.exp2(sc[i] - m)
            pb[i] = p.astype(BF)
            total = total + fold(jnp.sum, p)
        norm[...] = total
        acc[...] = acc[...] * alpha

    def weigh(n):
        for i, off in enumerate(planes(n)):
            acc[...] += dot(kv[1, at.plane(off)].reshape(512, HD), pb[i], TN)

    def og_cols(dp, plane):
        cols = pl.ds(pl.multiple_of(plane % 4 * 256, 256), 256)
        return ogf[dp * 2 + plane // 4, :, cols]

    def head_grad(off):
        plane = at.plane(off)
        links.wait(("sib", off), wf.at[:, plane, :, 1 - core], at.sibling())
        gacc[...] += sum(
            dot(og_cols(dp, plane), wf[dp, plane].reshape(256, 512)) for dp in (0, 1))

    def send_grad():
        ghs[...] = gacc[...].astype(BF)
        scatter_heads("g", lambda t: head(ghs, t), doh.at[j])

    def finish_attention():
        total = jnp.sum(norm[...], axis=0, keepdims=True)
        atth[...] = (acc[...] / total).T.astype(BF).reshape(4, 128, HD)
        lse[...] = top[0:1] + jnp.log2(total)
        scatter_heads("a", lambda t: atth.at[(j + t) % 4], head(att_tok, 0))

    def deltas():
        await_heads("g", doh.at[three_blocks])
        products = (doh[...].astype(F32) * atth[...].astype(F32)).reshape(512, HD)
        delta[...] = jnp.sum(products.T, axis=0, keepdims=True)

    def backward(off):
        plane = at.plane(off)
        qs = qh[...].reshape(512, HD)
        do = doh[...].reshape(512, HD)
        ks, vs = kv[0, plane].reshape(512, HD), kv[1, plane].reshape(512, HD)
        s = dot(ks, qs, NT) * SCALE2
        p = jnp.where(allowed(plane), jnp.exp2(s - lse[...]), 0.0)
        ds = (p * (dot(vs, do, NT) - delta[...])).astype(BF)
        dkv[1, plane] = dot(p.astype(BF), do).astype(BF).reshape(4, 128, HD)
        dkv[0, plane] = (dot(ds, qs) * SCALE).astype(BF).reshape(4, 128, HD)
        qacc[...] += dot(ks, ds, TN)

    def zsend(a, s, d):
        i = (1 - d) // 2
        p = at.plane(d * (4 - s))
        if s == 0 or (s == 1 and a != i):
            src = dkv.at[a, p]
        else:
            links.wait(("rz", a, d, s - 1), zr.at[a, i, s - 1], at.at_z(d))
            zs[a, i, s - 1] = plus(dkv[a, p], zr[a, i, s - 1]).astype(BF)
            src = zs.at[a, i, s - 1]
        links.send(("rz", a, d, s), src, zr.at[a, i, s], at.at_z(d))

    def zfinal(a):
        for i, d in SIDES:
            links.wait(("rz", a, d, 3), zr.at[a, i, 3], at.at_z(d))
        zfin[a] = plus(dkv[a, z], zr[a, 0, 3], zr[a, 1, 3]).astype(BF)
        scatter_heads(("dk", "dv")[a], lambda t: zfin.at[a, (j + t) % 4], head((dk, dv)[a], 0))

    def project(off):
        x = (mp + 4 + off) % 4
        rows = wf[x // 2, pl.ds(pl.multiple_of(x % 2 * 4, 4), 4)].reshape(1024, 512)
        px[x] = dot(att_tok[...], rows, NT).astype(BF)

    def xfirst():
        for i, d in SIDES:
            links.send(("x", d, 0), px.at[(mp + 2) % 4, pl.ds(i * 64, 64)], xr0.at[i], at.at_x(d))

    def xsecond(d):
        i = (1 - d) // 2
        chunk = (mp + 4 + d) % 4
        links.wait(("x", d, 0), xr0.at[i], at.at_x(d))
        xs[i, pl.ds(i * 64, 64)] = plus(px[chunk, pl.ds(i * 64, 64)], xr0[i]).astype(BF)
        xs[i, pl.ds(64 - i * 64, 64)] = px[chunk, pl.ds(64 - i * 64, 64)]
        links.send(("x", d, 1), xs.at[i], xr1.at[i], at.at_x(d))

    def xfinal():
        for i, d in SIDES:
            links.wait(("x", d, 1), xr1.at[i], at.at_x(d))
        projs[...] = plus(px[mp], xr1[0], xr1[1]).astype(BF)
        keep("proj", projs, proj)

    def await_attended():
        await_heads("a", att_tok.at[:, three_heads])

    def weight_grad(off):
        p = at.plane(off)
        for dp in (0, 1):
            part = dot(og_cols(dp, p), att_tok[...], TN).astype(BF)
            wgp[dp, p] = part.reshape(2, 2, 64, 512)
            links.send(("wsib", off), wgp.at[dp, p, :, 1 - core], sibr.at[dp, p], at.sibling())

    def yfirst(off):
        p = at.plane(off)
        links.wait(("wsib", off), sibr.at[:, p], at.sibling())
        for dp in (0, 1):
            for yhi in (0, 1):
                wsum[dp, p, yhi] = plus(wgp[dp, p, yhi, core], sibr[dp, p, yhi]).astype(BF)
        dp, yhi = at.yblock(2)
        for i, d in SIDES:
            links.send(("y", off, d, 0), wsum.at[dp, p, yhi, pl.ds(i * 32, 32)], yr0.at[p, i], at.at_y(d))

    def ysecond(off, d):
        p = at.plane(off)
        i = (1 - d) // 2
        dp, yhi = at.yblock(d)
        links.wait(("y", off, d, 0), yr0.at[p, i], at.at_y(d))
        rows = pl.ds(i * 32, 32)
        wsum[dp, p, yhi, rows] = plus(wsum[dp, p, yhi, rows], yr0[p, i]).astype(BF)
        links.send(("y", off, d, 1), wsum.at[dp, p, yhi], yr1.at[p, i], at.at_y(d))

    def yfinal(off):
        p = at.plane(off)
        for i, d in SIDES:
            links.wait(("y", off, d, 1), yr1.at[p, i], at.at_y(d))
        total = plus(wsum[at.dp, p, at.yhi], yr1[p, 0], yr1[p, 1])
        if off == 0:
            for i, d in SIDES:
                links.wait(("w", d, 3), wzr.at[i, 3], at.at_z(d))
            wgs[...] = plus(total, wzr[0, 3], wzr[1, 3])
            keep("wg", wgs, wg)
            return
        if off == 4:
            wyb[...] = total.astype(BF)
            for i, d in SIDES:
                rows = pl.ds(i * 32, 32)
                links.send(("w", d, 0), wyb.at[rows], wzr.at[i, 0, rows], at.at_z(d))
            return
        d = 1 if off > 0 else -1
        i = (1 - d) // 2
        s = 4 - abs(off)
        if s == 1:
            rows = pl.ds(i * 32, 32)
            links.wait(("w", d, 0), wzr.at[i, 0, rows], at.at_z(d))
            wzs[i, 0] = total.astype(BF)
            wzs[i, 0, rows] = plus(total[i * 32:i * 32 + 32], wzr[i, 0, rows]).astype(BF)
        else:
            links.wait(("w", d, s - 1), wzr.at[i, s - 1], at.at_z(d))
            wzs[i, s - 1] = plus(total, wzr[i, s - 1]).astype(BF)
        links.send(("w", d, s), wzs.at[i, s - 1], wzr.at[i, s], at.at_z(d))

    def send_dq():
        dqh[...] = (qacc[...] * SCALE).T.astype(BF).reshape(4, 128, HD)
        scatter_heads("dq", lambda t: dqh.at[(j + t) % 4], head(dq, 0))

    def finish():
        for name, out in (("dq", dq), ("dk", dk), ("dv", dv)):
            await_heads(name, out.at[:, three_heads])
        own["proj"].wait()
        own["wg"].wait()
        links.drain()

    tasks = {
        "K0": k0, "V0": v0, "Q0": q0, "W0": w0, "WY0": wy0, "OG0": og0, "RA": ring_start,
        "R": ring, "W": wstep, "WY": wy, "FY": wforward, "S": wshare, "OG": ogstep, "OL": oglast,
        "SC": scores, "WE": weigh, "HG": head_grad, "GH": send_grad, "FIN": finish_attention,
        "DEL": deltas, "B": backward, "Z": zsend, "ZF": zfinal, "PX": project, "XF": xfirst,
        "XS": xsecond, "XE": xfinal, "ATT": await_attended, "WG": weight_grad, "Y1": yfirst,
        "Y2": ysecond, "Y3": yfinal, "DQ": send_dq, "END": finish,
    }
    for name, *numbers in ORDER:
        tasks[name](*numbers)
    assert len(links.slots) == RECEIVES, len(links.slots)


def hand_over_kernel(*refs):
    for i in range(5):
        refs[5 + i][...] = refs[i][...]


def hand_over(*arrays):
    return pl.pallas_call(
        hand_over_kernel,
        out_shape=tuple(jax.ShapeDtypeStruct(a.shape, a.dtype) for a in arrays),
        in_specs=vmem(5),
        out_specs=tuple(vmem(5)),
        name="hand_over",
    )(*arrays)


def on_device(queries, key_rows, value_rows, out_weight, out_grad, block_offsets):
    heads = jax.ShapeDtypeStruct((128, 512), BF)
    proj, dq, dk, dv, wg = pl.pallas_call(
        kernel,
        out_shape=(
            jax.ShapeDtypeStruct((128, 1024), BF), heads, heads, heads,
            jax.ShapeDtypeStruct((64, 512), F32),
        ),
        in_specs=[pl.BlockSpec(memory_space=pltpu.SMEM)] + any_spec(5),
        out_specs=tuple(any_spec(5)),
        scratch_shapes=[
            pltpu.VMEM((4, 128, HD), BF),
            pltpu.VMEM((2, 8, 4, 128, HD), BF),
            pltpu.VMEM((2, 8, 2, 2, 64, 512), BF),
            pltpu.VMEM((4, 128, 1024), BF),
            pltpu.VMEM((4, 128, HD), BF),
            pltpu.VMEM((4, 128, HD), BF),
            pltpu.VMEM((128, 512), BF),
            pltpu.VMEM((128, 512), BF),
            pltpu.VMEM((4, 128, HD), BF),
            pltpu.VMEM((2, 8, 4, 128, HD), BF),
            pltpu.VMEM((4, 128, 1024), BF),
            pltpu.VMEM((2, 8, 2, 2, 64, 512), BF),
            pltpu.VMEM((2, 2, 4, 4, 128, HD), BF),
            pltpu.VMEM((2, 2, 3, 4, 128, HD), BF),
            pltpu.VMEM((2, 4, 128, HD), BF),
            pltpu.VMEM((2, 64, 1024), BF),
            pltpu.VMEM((2, 128, 1024), BF),
            pltpu.VMEM((2, 128, 1024), BF),
            pltpu.VMEM((128, 1024), BF),
            pltpu.VMEM((2, 8, 2, 64, 512), BF),
            pltpu.VMEM((2, 8, 2, 64, 512), BF),
            pltpu.VMEM((8, 2, 32, 512), BF),
            pltpu.VMEM((8, 2, 64, 512), BF),
            pltpu.VMEM((64, 512), BF),
            pltpu.VMEM((2, 4, 64, 512), BF),
            pltpu.VMEM((2, 3, 64, 512), BF),
            pltpu.VMEM((64, 512), F32),
            pltpu.VMEM((HD, 512), F32),
            pltpu.VMEM((8, 512), F32),
            pltpu.VMEM((8, 512), F32),
            pltpu.VMEM((2, 512, 512), F32),
            pltpu.VMEM((2, 512, 512), BF),
            pltpu.VMEM((128, 512), F32),
            pltpu.VMEM((1, 512), F32),
            pltpu.VMEM((1, 512), F32),
            pltpu.VMEM((1, 512), jnp.int32),
            pltpu.VMEM((HD, 512), F32),
            pltpu.SemaphoreType.DMA((SENDS,)),
            pltpu.SemaphoreType.DMA((RECEIVES,)),
            pltpu.SemaphoreType.DMA((12,)),
        ],
        compiler_params=pltpu.CompilerParams(
            collective_id=0, has_side_effects=True, vmem_limit_bytes=62 << 20),
        name="whole",
    )(block_offsets, queries[0], key_rows[0], value_rows[0], out_weight, out_grad[0])
    proj, dq, dk, dv, wg = hand_over(proj, dq, dk, dv, wg)
    return proj[None], dq[None], dk[None], dv[None], wg


def solution(mesh):
    tokens = P("dp", "ctx", "mp")
    features = P(("dp", "ctx"), "mp")
    return jax.shard_map(
        on_device,
        mesh=mesh,
        in_specs=(tokens, tokens, tokens, features, tokens, P("dp", None)),
        out_specs=(tokens, tokens, tokens, tokens, features),
        check_vma=False,
    )
```

time: 97.2 us -> 76.6 us (0.79)
  Pallas kernels: 91.1 us -> 75.2 us
  local copies, waits for them, and re-layouts: 5.21 us -> 0 us
    pallas_call x1, Pallas kernels: 91.1 us -> 73.2 us  [on_device(): pl.pallas_call(kernel, out_shape=(jax.ShapeDtypeStruct((128, 1024), BF),...]
    unnamed x13 -> x0, local copies, waits for them, and re-layouts: 5.21 us -> none
    pallas_call x0 -> x1, Pallas kernels: none -> 2.04 us  [hand_over(): pl.pallas_call(hand_over_kernel, out_shape=tuple((jax.ShapeDtypeStruct(a....]
where the time goes in v3:
time: 76.6 us; the launch traced here: 75.8 us
  Pallas kernels  75.2 us (98%)
    pallas_call x1, Pallas kernels, on_device(): pl.pallas_call(kernel, out_shape=(jax.ShapeDtypeStruct((128, 1024), BF),...  73.2 us
    pallas_call x1, Pallas kernels, hand_over(): pl.pallas_call(hand_over_kernel, out_shape=tuple((jax.ShapeDtypeStruct(a....  2.04 us

profile of v3, /device:TPU:1, one launch (start us, length us, event | category | flops | bytes accessed | tf_op | source)
XLA Modules:
  0.0 75.8 jit_solution(10694065232371543762)
XLA Ops:
  0.6 73.2 %whole.1 = (bf16[128,1024]{1,0:T(8,128)(2,1)}, bf16[128,512]{1,0:T(8,128)(2,1)}, bf16[128,512]{1,0:T(8,128)(2,1)}, bf16[128,512]{1,0:T(8,128)(2,1)}, f32[64,512]{1,0:T(8,128)}) custom-call(s32[1,32]{1,0:T(1,128)} %offsets.1, bf16[128,512]{1,0:T(8,128)(2,1)} %bitcast.9, bf16[128,512]{1,0:T(8,128)(2,1)} %bitcast.10, bf16[128,512]{1,0:T(8,128)(2,1)} %bitcast.11, ...), custom_call_target="tpu_custom_call" | custom-call | tf_op jit(solution)/shard_map/whole/pallas_call | solution.py:488
  73.8 2.0 %hand_over.1 = (bf16[128,1024]{1,0:T(8,128)(2,1)}, bf16[128,512]{1,0:T(8,128)(2,1)}, bf16[128,512]{1,0:T(8,128)(2,1)}, bf16[128,512]{1,0:T(8,128)(2,1)}, f32[64,512]{1,0:T(8,128)}) custom-call(bf16[128,1024]{1,0:T(8,128)(2,1)} %get-tuple-element.15.refs_0_, bf16[128,512]{1,0:T(8,128)(2,1)} %get-tuple-element.16.refs_1_, ...), custom_call_target="tpu_custom_call" | custom-call | tf_op jit(solution)/shard_map/hand_over/pallas_call | solution.py:477

commit v4 on v3

--- a/solution.py
+++ b/solution.py
@@ -100,40 +100,43 @@
 TN = (((0,), (0,)), ((), ()))
 SIDES = ((0, 1), (1, -1))
 SENDS = 32
-RECEIVES = 131
+RECEIVES = 121
 ORDER = (
-    ("K0",), ("W0",), ("WY0",), ("Q0",), ("W", 0, -1),
-    ("W", 0, 1), ("OG0",), ("V0",), ("WY", 1), ("WY", -1),
-    ("RA", 0), ("W", 1, 1), ("FY", 0, 1), ("FY", 0, -1), ("W", 1, -1),
-    ("WY", 2), ("WY", -2), ("RA", 1), ("W", 2, -1), ("W", 2, 1),
-    ("R", 0, 0, -1), ("WY", -3), ("SC", 0), ("R", 0, 0, 1), ("FY", 1, -1),
-    ("FY", -2, 1), ("WY", 3), ("OG", 1), ("R", 1, 0, 1), ("W", 3, -1),
-    ("FY", 2, 1), ("FY", -1, -1), ("FY", -1, 1), ("R", 1, 0, -1), ("W", 3, 1),
-    ("OG", -1), ("WE", 0), ("FY", -2, -1), ("FY", 1, 1), ("SC", 1),
-    ("FY", -3, -1), ("R", 0, 1, -1), ("WY", 4), ("S", 0), ("R", 0, 1, 1),
-    ("FY", 2, -1), ("FY", -3, 1), ("WE", 1), ("S", -1), ("FY", 3, -1),
-    ("FY", 3, 1), ("R", 1, 1, 1), ("FY", 4, -1), ("S", -2), ("R", 1, 1, -1),
-    ("FY", 4, 1), ("S", 2), ("SC", 2), ("OL",), ("HG", -2),
-    ("S", -3), ("S", 3), ("S", 1), ("HG", 2), ("R", 0, 2, 1),
-    ("HG", 0), ("S", 4), ("HG", -1), ("R", 0, 2, -1), ("HG", -3),
-    ("R", 1, 2, -1), ("WE", 2), ("HG", 1), ("HG", 4), ("HG", 3),
-    ("GH",), ("R", 1, 2, 1), ("SC", 3), ("R", 0, 3, 1), ("WE", 3),
+    ("K0",), ("W0",), ("V0",), ("RS", 0, 1), ("RO", 0, -1),
+    ("WY0",), ("Q0",), ("RO", 1, 1), ("RO", 0, 1), ("RO", 1, -1),
+    ("RS", 0, -1), ("W", 0, 1), ("RS", 1, -1), ("W", 0, -1), ("WY", 1),
+    ("RA", 0, 1), ("OG0",), ("RA", 1, -1), ("WY", -1), ("RS", 1, 1),
+    ("RA", 0, -1), ("W", 1, 1), ("WY", -2), ("W", 1, -1), ("WY", 2),
+    ("RA", 1, 1), ("R", 0, 0, 1), ("FY", 0, -1), ("R", 1, 0, -1), ("W", 2, 1),
+    ("WY", -3), ("W", 2, -1), ("WY", 3), ("FY", -1, -1), ("FY", -2, -1),
+    ("R", 1, 0, 1), ("FY", -2, 1), ("SC", 0), ("FY", 0, 1), ("FY", -1, 1),
+    ("WE", 0), ("R", 0, 0, -1), ("SC", 1), ("FY", 1, -1), ("R", 1, 1, -1),
+    ("W", 3, 1), ("W", 3, -1), ("R", 0, 1, 1), ("WY", 4), ("OG", -1),
+    ("OG", 1), ("FY", 3, 1), ("FY", 3, -1), ("S", -2), ("FY", 1, 1),
+    ("S", 0), ("FY", -3, 1), ("R", 1, 1, 1), ("FY", -3, -1), ("FY", 2, 1),
+    ("FY", 2, -1), ("R", 0, 1, -1), ("WE", 1), ("SC", 2), ("FY", 4, 1),
+    ("FY", 4, -1), ("S", -1), ("WE", 2), ("S", 3), ("R", 0, 2, 1),
+    ("S", -3), ("S", 1), ("OL",), ("HG", -2), ("HG", -1),
+    ("R", 1, 2, -1), ("S", 2), ("HG", 0), ("S", 4), ("HG", 3),
+    ("HG", -3), ("HG", 1), ("HG", 2), ("HG", 4), ("GH",),
+    ("R", 0, 2, -1), ("SC", 3), ("R", 1, 2, 1), ("WE", 3), ("R", 0, 3, 1),
     ("SC", 4), ("R", 1, 3, -1), ("WE", 4), ("FIN",), ("DEL",),
-    ("B", 4), ("Z", 1, 0, -1), ("Z", 0, 0, 1), ("B", 3), ("B", -3),
-    ("Z", 0, 1, -1), ("Z", 1, 1, 1), ("B", 2), ("ATT",), ("WG", 4),
-    ("WG", 3), ("WG", -3), ("WG", 2), ("B", -2), ("Y1", 4),
-    ("Z", 1, 1, -1), ("Z", 0, 1, 1), ("WG", -2), ("Y1", -3), ("Y1", 3),
-    ("WG", -1), ("Y1", 2), ("WG", 1), ("Z", 0, 2, -1), ("Y1", -2),
-    ("Z", 1, 2, 1), ("Y2", 4, 1), ("WG", 0), ("Y2", 4, -1), ("PX", 2),
-    ("Y2", -3, 1), ("Y1", -1), ("Y2", -3, -1), ("Y1", 1), ("Z", 1, 2, -1),
-    ("Z", 0, 2, 1), ("Y2", 3, -1), ("PX", 1), ("B", -1), ("XF",),
-    ("Y2", 3, 1), ("B", 1), ("Y3", 4), ("Z", 0, 3, -1), ("Y2", -2, 1),
-    ("Z", 1, 3, 1), ("Y2", 2, 1), ("Y1", 0), ("Y2", -2, -1), ("B", 0),
-    ("Y2", 1, 1), ("Y2", 2, -1), ("DQ",), ("Y2", -1, 1), ("Y3", -3),
-    ("Y3", 3), ("PX", -1), ("Y2", 1, -1), ("Z", 1, 3, -1), ("XS", -1),
-    ("Z", 0, 3, 1), ("XS", 1), ("Y2", -1, -1), ("Y2", 0, -1), ("Y2", 0, 1),
-    ("Y3", 2), ("Y3", -2), ("ZF", 1), ("PX", 0), ("ZF", 0),
-    ("Y3", -1), ("Y3", 1), ("XE",), ("Y3", 0), ("END",),
+    ("BH", 0), ("ZH", 0, 1), ("ZH", 0, -1), ("BH", 1), ("ZH", 1, 1),
+    ("ZH", 1, -1), ("B", -3), ("B", 3), ("Z", 1, 1, 1), ("Z", 0, 1, -1),
+    ("ATT",), ("WG", -3), ("WG", 1), ("WG", 4), ("WG", 3),
+    ("WG", 2), ("B", 2), ("Y1", -3), ("Z", 1, 1, -1), ("Z", 0, 1, 1),
+    ("Y1", 4), ("Y1", 3), ("Y1", 2), ("Y1", 1), ("B", -2),
+    ("Z", 0, 2, -1), ("Z", 1, 2, 1), ("Y2", -3, 1), ("Y2", -3, -1), ("WG", -2),
+    ("Y2", 4, -1), ("PX", 2), ("XF",), ("Y2", 4, 1), ("WG", -1),
+    ("WG", 0), ("Z", 0, 2, 1), ("Z", 1, 2, -1), ("Y2", 2, -1), ("Y1", -2),
+    ("Y2", 2, 1), ("Y2", 3, -1), ("Y2", 1, -1), ("B", 1), ("Y2", 3, 1),
+    ("Y1", -1), ("Y3", 4), ("Z", 1, 3, 1), ("Y1", 0), ("Y2", 1, 1),
+    ("B", -1), ("Z", 1, 3, -1), ("Y2", -2, 1), ("PX", 1), ("PX", -1),
+    ("XS", 1), ("Y2", -2, -1), ("Y3", 3), ("Y3", -3), ("XS", -1),
+    ("Y2", -1, 1), ("Z", 0, 3, -1), ("Z", 0, 3, 1), ("Y2", -1, -1), ("B", 0),
+    ("DQ",), ("Y2", 0, -1), ("Y3", 2), ("ZF", 1), ("Y2", 0, 1),
+    ("Y3", -2), ("ZF", 0), ("Y3", 1), ("Y3", -1), ("PX", 0),
+    ("XE",), ("Y3", 0), ("END",),
 )
 
 
@@ -178,6 +181,14 @@
             links.send(name, blocks(t), dst, at.at_j(t))
         keep(name, blocks(0), dst)
 
+    def scatter_kv(a, ref):
+        dst = kv.at[a, z, j]
+        for c in (0, 1):
+            to = 2 - 2 * at.yhi + c
+            links.send(("kv", a), head(ref, to - j), dst, {"ctx": z * 4 + to})
+        links.send(("kvs", a), head(ref, 1 - 2 * core), dst, at.sibling())
+        keep("kv"[a], head(ref, 0), dst)
+
     def await_heads(name, three):
         links.wait(name, three, at.at_j(1))
         own[name].wait()
@@ -186,10 +197,10 @@
     three_heads = pl.ds(0, 3 * HD)
 
     def k0():
-        scatter_heads("k", lambda t: head(k, t), kv.at[0, z, j])
+        scatter_kv(0, k)
 
     def v0():
-        scatter_heads("v", lambda t: head(v, t), kv.at[1, z, j])
+        scatter_kv(1, v)
 
     def q0():
         scatter_heads("q", lambda t: head(q, t), qh.at[j])
@@ -208,10 +219,28 @@
             links.send(("og", d, 0), og, ogf.at[mp], at.at_x(d))
         keep("og", og, ogf.at[mp])
 
-    def ring_start(a):
-        await_heads("kv"[a], kv.at[a, z, three_blocks])
-        for d in (1, -1):
-            links.send(("z", a, d, 0), kv.at[a, z], kv.at[a, z], at.at_z(d))
+    met = set()
+
+    def first(*names):
+        fresh = names not in met
+        met.add(names)
+        return fresh
+
+    def ring_own(a, d):
+        links.send(("z", a, d, 0), head((k, v)[a], 0), kv.at[a, z, j], at.at_z(d))
+
+    def ring_sibling(a, d):
+        block = kv.at[a, z, j + 1 - 2 * core]
+        if first("sibling", a):
+            links.wait(("kvs", a), block, at.sibling())
+        links.send(("z", a, d, 0), block, block, at.at_z(d))
+
+    def ring_start(a, d):
+        pair = kv.at[a, z, pl.ds(2 - 2 * at.yhi, 2)]
+        if first("pair", a):
+            links.wait(("kv", a), pair, at.at_j(2))
+            own["kv"[a]].wait()
+        links.send(("z", a, d, 0), pair, pair, at.at_z(d))
 
     def ring(a, s, d):
         i = (1 - d) // 2
@@ -259,9 +288,10 @@
 
     row_in = lax.broadcasted_iota(jnp.int32, (128, 512), 0)
 
-    def allowed(plane):
+    def allowed(plane, start=0, blocks=4):
         return jnp.concatenate(
-            [row_in <= posq[...] - offsets[0, plane * 4 + i] * 128 for i in range(4)], axis=0)
+            [row_in <= posq[...] - offsets[0, plane * 4 + start + i] * 128 for i in range(blocks)],
+            axis=0)
 
     def fold(op, rows):
         return op(rows.reshape(64, 8, 512), axis=0)
@@ -333,32 +363,44 @@
         products = (doh[...].astype(F32) * atth[...].astype(F32)).reshape(512, HD)
         delta[...] = jnp.sum(products.T, axis=0, keepdims=True)
 
-    def backward(off):
+    def backward_rows(off, first_block, blocks):
         plane = at.plane(off)
+        some = pl.ds(first_block, blocks)
         qs = qh[...].reshape(512, HD)
         do = doh[...].reshape(512, HD)
-        ks, vs = kv[0, plane].reshape(512, HD), kv[1, plane].reshape(512, HD)
+        ks = kv[0, plane, some].reshape(blocks * 128, HD)
+        vs = kv[1, plane, some].reshape(blocks * 128, HD)
         s = dot(ks, qs, NT) * SCALE2
-        p = jnp.where(allowed(plane), jnp.exp2(s - lse[...]), 0.0)
+        p = jnp.where(allowed(plane, first_block, blocks), jnp.exp2(s - lse[...]), 0.0)
         ds = (p * (dot(vs, do, NT) - delta[...])).astype(BF)
-        dkv[1, plane] = dot(p.astype(BF), do).astype(BF).reshape(4, 128, HD)
-        dkv[0, plane] = (dot(ds, qs) * SCALE).astype(BF).reshape(4, 128, HD)
+        dkv[1, plane, some] = dot(p.astype(BF), do).astype(BF).reshape(blocks, 128, HD)
+        dkv[0, plane, some] = (dot(ds, qs) * SCALE).astype(BF).reshape(blocks, 128, HD)
         qacc[...] += dot(ks, ds, TN)
 
+    def backward(off):
+        backward_rows(off, 0, 4)
+
+    def backward_half(h):
+        backward_rows(4, h * 2, 2)
+
+    def zhalf(h, d):
+        i = (1 - d) // 2
+        half = pl.ds(h * 2, 2)
+        links.send(("rz", i, d, 0), dkv.at[i, at.plane(4), half], zr.at[i, i, 0, half], at.at_z(d))
+
     def zsend(a, s, d):
         i = (1 - d) // 2
         p = at.plane(d * (4 - s))
-        if s == 0 or (s == 1 and a != i):
+        if s == 1 and a != i:
             src = dkv.at[a, p]
         else:
             links.wait(("rz", a, d, s - 1), zr.at[a, i, s - 1], at.at_z(d))
             zs[a, i, s - 1] = plus(dkv[a, p], zr[a, i, s - 1]).astype(BF)
             src = zs.at[a, i, s - 1]
-        links.send(("rz", a, d, s), src, zr.at[a, i, s], at.at_z(d))
+        links.send(("rz", a, d, s) if s < 3 else ("rz", a, 3), src, zr.at[a, i, s], at.at_z(d))
 
     def zfinal(a):
-        for i, d in SIDES:
-            links.wait(("rz", a, d, 3), zr.at[a, i, 3], at.at_z(d))
+        links.wait(("rz", a, 3), zr.at[a, :, 3], at.at_z(1))
         zfin[a] = plus(dkv[a, z], zr[a, 0, 3], zr[a, 1, 3]).astype(BF)
         scatter_heads(("dk", "dv")[a], lambda t: zfin.at[a, (j + t) % 4], head((dk, dv)[a], 0))
 
@@ -377,11 +419,10 @@
         links.wait(("x", d, 0), xr0.at[i], at.at_x(d))
         xs[i, pl.ds(i * 64, 64)] = plus(px[chunk, pl.ds(i * 64, 64)], xr0[i]).astype(BF)
         xs[i, pl.ds(64 - i * 64, 64)] = px[chunk, pl.ds(64 - i * 64, 64)]
-        links.send(("x", d, 1), xs.at[i], xr1.at[i], at.at_x(d))
+        links.send("xlast", xs.at[i], xr1.at[i], at.at_x(d))
 
     def xfinal():
-        for i, d in SIDES:
-            links.wait(("x", d, 1), xr1.at[i], at.at_x(d))
+        links.wait("xlast", xr1, at.at_x(1))
         projs[...] = plus(px[mp], xr1[0], xr1[1]).astype(BF)
         keep("proj", projs, proj)
 
@@ -412,16 +453,14 @@
         links.wait(("y", off, d, 0), yr0.at[p, i], at.at_y(d))
         rows = pl.ds(i * 32, 32)
         wsum[dp, p, yhi, rows] = plus(wsum[dp, p, yhi, rows], yr0[p, i]).astype(BF)
-        links.send(("y", off, d, 1), wsum.at[dp, p, yhi], yr1.at[p, i], at.at_y(d))
+        links.send(("ylast", off), wsum.at[dp, p, yhi], yr1.at[p, i], at.at_y(d))
 
     def yfinal(off):
         p = at.plane(off)
-        for i, d in SIDES:
-            links.wait(("y", off, d, 1), yr1.at[p, i], at.at_y(d))
+        links.wait(("ylast", off), yr1.at[p], at.at_y(1))
         total = plus(wsum[at.dp, p, at.yhi], yr1[p, 0], yr1[p, 1])
         if off == 0:
-            for i, d in SIDES:
-                links.wait(("w", d, 3), wzr.at[i, 3], at.at_z(d))
+            links.wait("wlast", wzr.at[:, 3], at.at_z(1))
             wgs[...] = plus(total, wzr[0, 3], wzr[1, 3])
             keep("wg", wgs, wg)
             return
@@ -442,7 +481,7 @@
         else:
             links.wait(("w", d, s - 1), wzr.at[i, s - 1], at.at_z(d))
             wzs[i, s - 1] = plus(total, wzr[i, s - 1]).astype(BF)
-        links.send(("w", d, s), wzs.at[i, s - 1], wzr.at[i, s], at.at_z(d))
+        links.send(("w", d, s) if s < 3 else "wlast", wzs.at[i, s - 1], wzr.at[i, s], at.at_z(d))
 
     def send_dq():
         dqh[...] = (qacc[...] * SCALE).T.astype(BF).reshape(4, 128, HD)
@@ -456,7 +495,7 @@
         links.drain()
 
     tasks = {
-        "K0": k0, "V0": v0, "Q0": q0, "W0": w0, "WY0": wy0, "OG0": og0, "RA": ring_start,
+        "K0": k0, "V0": v0, "Q0": q0, "W0": w0, "WY0": wy0, "OG0": og0, "RA": ring_start, "RO": ring_own, "RS": ring_sibling, "BH": backward_half, "ZH": zhalf,
         "R": ring, "W": wstep, "WY": wy, "FY": wforward, "S": wshare, "OG": ogstep, "OL": oglast,
         "SC": scores, "WE": weigh, "HG": head_grad, "GH": send_grad, "FIN": finish_attention,
         "DEL": deltas, "B": backward, "Z": zsend, "ZF": zfinal, "PX": project, "XF": xfirst,

time: 76.6 us -> 74.6 us (0.974)
  Pallas kernels: 75.2 us -> 73.9 us
    pallas_call x1, Pallas kernels: 73.2 us -> 71.8 us  [on_device(): pl.pallas_call(kernel, out_shape=(jax.ShapeDtypeStruct((128, 1024), BF),...]
where the time goes in v4:
time: 74.6 us; the launch traced here: 74.5 us
  Pallas kernels  73.9 us (99%)
    pallas_call x1, Pallas kernels, on_device(): pl.pallas_call(kernel, out_shape=(jax.ShapeDtypeStruct((128, 1024), BF),...  71.8 us
    pallas_call x1, Pallas kernels, hand_over(): pl.pallas_call(hand_over_kernel, out_shape=tuple((jax.ShapeDtypeStruct(a....  2.04 us

profile of v4, /device:TPU:1, one launch (start us, length us, event | category | flops | bytes accessed | tf_op | source)
XLA Modules:
  0.0 74.5 jit_solution(14127910302087818310)
XLA Ops:
  0.6 71.8 %whole.1 = (bf16[128,1024]{1,0:T(8,128)(2,1)}, bf16[128,512]{1,0:T(8,128)(2,1)}, bf16[128,512]{1,0:T(8,128)(2,1)}, bf16[128,512]{1,0:T(8,128)(2,1)}, f32[64,512]{1,0:T(8,128)}) custom-call(s32[1,32]{1,0:T(1,128)} %offsets.1, bf16[128,512]{1,0:T(8,128)(2,1)} %bitcast.9, bf16[128,512]{1,0:T(8,128)(2,1)} %bitcast.10, bf16[128,512]{1,0:T(8,128)(2,1)} %bitcast.11, ...), custom_call_target="tpu_custom_call" | custom-call | tf_op jit(solution)/shard_map/whole/pallas_call | solution.py:527
  72.5 2.0 %hand_over.1 = (bf16[128,1024]{1,0:T(8,128)(2,1)}, bf16[128,512]{1,0:T(8,128)(2,1)}, bf16[128,512]{1,0:T(8,128)(2,1)}, bf16[128,512]{1,0:T(8,128)(2,1)}, f32[64,512]{1,0:T(8,128)}) custom-call(bf16[128,1024]{1,0:T(8,128)(2,1)} %get-tuple-element.15.refs_0_, bf16[128,512]{1,0:T(8,128)(2,1)} %get-tuple-element.16.refs_1_, ...), custom_call_target="tpu_custom_call" | custom-call | tf_op jit(solution)/shard_map/hand_over/pallas_call | solution.py:516

commit v5 on v4

--- a/solution.py
+++ b/solution.py
@@ -102,40 +102,40 @@
 SENDS = 32
 RECEIVES = 121
 ORDER = (
-    ("K0",), ("W0",), ("V0",), ("RS", 0, 1), ("RO", 0, -1),
-    ("WY0",), ("Q0",), ("RO", 1, 1), ("RO", 0, 1), ("RO", 1, -1),
-    ("RS", 0, -1), ("W", 0, 1), ("RS", 1, -1), ("W", 0, -1), ("WY", 1),
-    ("RA", 0, 1), ("OG0",), ("RA", 1, -1), ("WY", -1), ("RS", 1, 1),
-    ("RA", 0, -1), ("W", 1, 1), ("WY", -2), ("W", 1, -1), ("WY", 2),
-    ("RA", 1, 1), ("R", 0, 0, 1), ("FY", 0, -1), ("R", 1, 0, -1), ("W", 2, 1),
-    ("WY", -3), ("W", 2, -1), ("WY", 3), ("FY", -1, -1), ("FY", -2, -1),
-    ("R", 1, 0, 1), ("FY", -2, 1), ("SC", 0), ("FY", 0, 1), ("FY", -1, 1),
-    ("WE", 0), ("R", 0, 0, -1), ("SC", 1), ("FY", 1, -1), ("R", 1, 1, -1),
-    ("W", 3, 1), ("W", 3, -1), ("R", 0, 1, 1), ("WY", 4), ("OG", -1),
-    ("OG", 1), ("FY", 3, 1), ("FY", 3, -1), ("S", -2), ("FY", 1, 1),
-    ("S", 0), ("FY", -3, 1), ("R", 1, 1, 1), ("FY", -3, -1), ("FY", 2, 1),
-    ("FY", 2, -1), ("R", 0, 1, -1), ("WE", 1), ("SC", 2), ("FY", 4, 1),
-    ("FY", 4, -1), ("S", -1), ("WE", 2), ("S", 3), ("R", 0, 2, 1),
-    ("S", -3), ("S", 1), ("OL",), ("HG", -2), ("HG", -1),
-    ("R", 1, 2, -1), ("S", 2), ("HG", 0), ("S", 4), ("HG", 3),
-    ("HG", -3), ("HG", 1), ("HG", 2), ("HG", 4), ("GH",),
-    ("R", 0, 2, -1), ("SC", 3), ("R", 1, 2, 1), ("WE", 3), ("R", 0, 3, 1),
-    ("SC", 4), ("R", 1, 3, -1), ("WE", 4), ("FIN",), ("DEL",),
-    ("BH", 0), ("ZH", 0, 1), ("ZH", 0, -1), ("BH", 1), ("ZH", 1, 1),
-    ("ZH", 1, -1), ("B", -3), ("B", 3), ("Z", 1, 1, 1), ("Z", 0, 1, -1),
-    ("ATT",), ("WG", -3), ("WG", 1), ("WG", 4), ("WG", 3),
-    ("WG", 2), ("B", 2), ("Y1", -3), ("Z", 1, 1, -1), ("Z", 0, 1, 1),
-    ("Y1", 4), ("Y1", 3), ("Y1", 2), ("Y1", 1), ("B", -2),
-    ("Z", 0, 2, -1), ("Z", 1, 2, 1), ("Y2", -3, 1), ("Y2", -3, -1), ("WG", -2),
-    ("Y2", 4, -1), ("PX", 2), ("XF",), ("Y2", 4, 1), ("WG", -1),
-    ("WG", 0), ("Z", 0, 2, 1), ("Z", 1, 2, -1), ("Y2", 2, -1), ("Y1", -2),
-    ("Y2", 2, 1), ("Y2", 3, -1), ("Y2", 1, -1), ("B", 1), ("Y2", 3, 1),
-    ("Y1", -1), ("Y3", 4), ("Z", 1, 3, 1), ("Y1", 0), ("Y2", 1, 1),
-    ("B", -1), ("Z", 1, 3, -1), ("Y2", -2, 1), ("PX", 1), ("PX", -1),
-    ("XS", 1), ("Y2", -2, -1), ("Y3", 3), ("Y3", -3), ("XS", -1),
-    ("Y2", -1, 1), ("Z", 0, 3, -1), ("Z", 0, 3, 1), ("Y2", -1, -1), ("B", 0),
-    ("DQ",), ("Y2", 0, -1), ("Y3", 2), ("ZF", 1), ("Y2", 0, 1),
-    ("Y3", -2), ("ZF", 0), ("Y3", 1), ("Y3", -1), ("PX", 0),
+    ("K0",), ("W0",), ("V0",), ("RS", 1, 1), ("Q0",),
+    ("RS", 0, -1), ("RS", 1, -1), ("RO", 1, -1), ("RO", 1, 1), ("RS", 0, 1),
+    ("OG0",), ("W", 0, 1), ("WY", -1), ("WY0",), ("RO", 0, -1),
+    ("RA", 0, 1), ("RO", 0, 1), ("W", 0, -1), ("WY", 1), ("RA", 1, -1),
+    ("RA", 0, -1), ("W", 1, 1), ("WY", -2), ("RA", 1, 1), ("W", 1, -1),
+    ("WY", 2), ("R", 0, 0, 1), ("R", 1, 0, -1), ("FY", 0, -1), ("W", 2, 1),
+    ("WY", -3), ("FY", -2, 1), ("FY", -2, -1), ("R", 1, 0, 1), ("W", 2, -1),
+    ("WY", 3), ("SC", 0), ("WE", 0), ("OG", 1), ("FY", -1, 1),
+    ("FY", 0, 1), ("R", 0, 0, -1), ("FY", -1, -1), ("W", 3, 1), ("W", 3, -1),
+    ("WY", 4), ("R", 0, 1, 1), ("R", 1, 1, -1), ("FY", -3, 1), ("FY", 3, 1),
+    ("FY", -3, -1), ("FY", 2, -1), ("OG", -1), ("SC", 1), ("WE", 1),
+    ("FY", 2, 1), ("FY", 3, -1), ("FY", 1, 1), ("FY", 1, -1), ("S", -2),
+    ("R", 1, 1, 1), ("R", 0, 1, -1), ("FY", 4, 1), ("S", 0), ("FY", 4, -1),
+    ("S", -1), ("S", -3), ("SC", 2), ("R", 0, 2, 1), ("S", 2),
+    ("S", 3), ("R", 1, 2, -1), ("S", 1), ("OL",), ("HG", 0),
+    ("S", 4), ("HG", -3), ("HG", -2), ("HG", -1), ("HG", 2),
+    ("HG", 3), ("HG", 1), ("HG", 4), ("GH",), ("WE", 2),
+    ("R", 0, 2, -1), ("SC", 3), ("R", 1, 2, 1), ("WE", 3), ("R", 1, 3, -1),
+    ("R", 0, 3, 1), ("SC", 4), ("WE", 4), ("FIN",), ("DEL",),
+    ("BH", 0), ("ZH", 0, 1), ("ZH", 0, -1), ("BH", 1), ("ZH", 1, -1),
+    ("ZH", 1, 1), ("B", -3), ("Z", 0, 1, -1), ("B", 3), ("Z", 1, 1, 1),
+    ("ATT",), ("WG", 4), ("WG", -3), ("WG", 2), ("WG", 3),
+    ("PX", 2), ("WG", 1), ("XF",), ("WG", 0), ("WG", -1),
+    ("Y1", 4), ("Z", 1, 1, -1), ("Z", 0, 1, 1), ("Y1", -3), ("WG", -2),
+    ("Y1", 1), ("Y1", 3), ("B", 2), ("Y2", 4, -1), ("Y2", 4, 1),
+    ("Z", 1, 2, 1), ("B", -2), ("Z", 0, 2, -1), ("Y1", 2), ("Y1", -2),
+    ("Y1", -1), ("Z", 0, 2, 1), ("Y1", 0), ("Y3", 4), ("Y2", -3, -1),
+    ("Y2", -3, 1), ("Z", 1, 2, -1), ("B", 1), ("Z", 1, 3, 1), ("Y2", 3, 1),
+    ("Y2", 3, -1), ("Y2", -2, -1), ("Y2", -2, 1), ("B", -1), ("Z", 0, 3, -1),
+    ("Y2", 2, -1), ("PX", -1), ("Y2", 2, 1), ("PX", 1), ("XS", 1),
+    ("Y3", -3), ("Y2", 1, -1), ("Y2", 0, -1), ("Y3", 3), ("Y2", -1, -1),
+    ("Z", 0, 3, 1), ("Z", 1, 3, -1), ("Y2", 0, 1), ("PX", 0), ("Y2", 1, 1),
+    ("XS", -1), ("B", 0), ("DQ",), ("Y3", 2), ("Y2", -1, 1),
+    ("Y3", -2), ("ZF", 0), ("ZF", 1), ("Y3", 1), ("Y3", -1),
     ("XE",), ("Y3", 0), ("END",),
 )
 

time: 74.6 us -> 77.2 us (1.035); the launches traced: 74.5 us -> 75.8 us
  Pallas kernels: 73.9 us -> 75.2 us
    pallas_call x1, Pallas kernels: 71.8 us -> 73.1 us  [on_device(): pl.pallas_call(kernel, out_shape=(jax.ShapeDtypeStruct((128, 1024), BF),...]
where the time goes in v5:
time: 77.2 us; the launch traced here: 75.8 us
  Pallas kernels  75.2 us (97%)
    pallas_call x1, Pallas kernels, on_device(): pl.pallas_call(kernel, out_shape=(jax.ShapeDtypeStruct((128, 1024), BF),...  73.1 us
    pallas_call x1, Pallas kernels, hand_over(): pl.pallas_call(hand_over_kernel, out_shape=tuple((jax.ShapeDtypeStruct(a....  2.04 us

profile of v5, /device:TPU:1, one launch (start us, length us, event | category | flops | bytes accessed | tf_op | source)
XLA Modules:
  0.0 75.8 jit_solution(12397383664700102970)
XLA Ops:
  0.6 73.1 %whole.1 = (bf16[128,1024]{1,0:T(8,128)(2,1)}, bf16[128,512]{1,0:T(8,128)(2,1)}, bf16[128,512]{1,0:T(8,128)(2,1)}, bf16[128,512]{1,0:T(8,128)(2,1)}, f32[64,512]{1,0:T(8,128)}) custom-call(s32[1,32]{1,0:T(1,128)} %offsets.1, bf16[128,512]{1,0:T(8,128)(2,1)} %bitcast.9, bf16[128,512]{1,0:T(8,128)(2,1)} %bitcast.10, bf16[128,512]{1,0:T(8,128)(2,1)} %bitcast.11, ...), custom_call_target="tpu_custom_call" | custom-call | tf_op jit(solution)/shard_map/whole/pallas_call | solution.py:527
  73.8 2.0 %hand_over.1 = (bf16[128,1024]{1,0:T(8,128)(2,1)}, bf16[128,512]{1,0:T(8,128)(2,1)}, bf16[128,512]{1,0:T(8,128)(2,1)}, bf16[128,512]{1,0:T(8,128)(2,1)}, f32[64,512]{1,0:T(8,128)}) custom-call(bf16[128,1024]{1,0:T(8,128)(2,1)} %get-tuple-element.15.refs_0_, bf16[128,512]{1,0:T(8,128)(2,1)} %get-tuple-element.16.refs_1_, ...), custom_call_target="tpu_custom_call" | custom-call | tf_op jit(solution)/shard_map/hand_over/pallas_call | solution.py:516
